TPU v7x, 256 devices: a whole 4x4x8 slice. The times are simulated.
256 devices in a mesh: row: 8 (over x, z_hi), col: 32 (over z_lo, y, core).
Axes of the slice: x: 4, y: 4, z: 8 (z_hi: 2, z_lo: 4; z = z_hi * 4 + z_lo), core: 2. Of those that a mesh axis runs over, the one named last changes fastest.
Arguments:
- src_feat: bfloat16 [131072, 128], P('col'), may hold values from -68 to 68
- dst_feat: bfloat16 [16384, 128], P(('row', 'col')), may hold values from -6 to 6
- weight: bfloat16 [128, 512], replicated, may hold values from -0.5 to 0.5
- att_src: float32 [8, 64], replicated, may hold values from -4 to 4
- att_dst: float32 [8, 64], replicated, may hold values from -4 to 4
- bias: float32 [512], replicated, may hold values from -3 to 3
- tile_rows: int32 [8, 32, 160], P('row', 'col'), may hold values from 0 to 15
- tile_cols: int32 [8, 32, 160], P('row', 'col'), may hold values from 0 to 31
- tile_masks: int32 [8, 32, 160, 128, 128], P('row', 'col'), may hold values 0 or 1
- tile_count: int32 [8, 32], P('row', 'col'), may hold values from 40 to 160, as said below
Outputs:
- node_out: float32 [16384, 512], P(('row', 'col'))
Inputs may be any that keep to these rules, and one draw needn't show every extreme that they name: Device (r, c) uses its first tile_count[r, c] tile slots; later slots hold arbitrary entries that are not part of the graph; some device uses all 160 slots.
All inputs are finite; a program needn't handle non-finite values. No bound on the sum of `tile_masks` on one device may be relied on, other than what follows from the above.
Results may differ from a plain program's by a relative error of at most 0.0042.
Values may be sent and summed in bfloat16 or wider, within the bound.
A program may use at most 128 MiB of HBM per device.

v0:
```python
import jax
import jax.numpy as jnp
from jax import lax
from jax.sharding import PartitionSpec as P

HEADS = 8
HEAD_DIM = 64
TILE = 128


NEG_FILL = -1e30


def leaky_relu(values):
    return jnp.where(values > 0, values, 0.2 * values)


def project_rows(features, weight):
    values = jnp.dot(features, weight, preferred_element_type=jnp.float32).astype(jnp.bfloat16)
    return lax.optimization_barrier(values)


def head_scores(values, attention):
    row_count = values.shape[0]
    wide = values.astype(jnp.float32).reshape(row_count, HEADS, HEAD_DIM)
    return jnp.sum(wide * attention[None], axis=2)


def tile_update(carry_state, dst_scores, src_scores, src_values, tile_mask, row_start, col_start):
    run_max, run_sum, run_acc = carry_state
    dst_part = lax.dynamic_slice_in_dim(dst_scores, row_start, TILE, 1)
    src_part = lax.dynamic_slice_in_dim(src_scores, col_start, TILE, 1)
    logits = leaky_relu(dst_part[:, :, None] + src_part[:, None, :])
    present = tile_mask[None] > 0
    logits = jnp.where(present, logits, NEG_FILL)
    old_max = lax.dynamic_slice_in_dim(run_max, row_start, TILE, 1)
    new_max = jnp.maximum(old_max, jnp.max(logits, axis=2))
    probs = jnp.where(present, jnp.exp(logits - new_max[:, :, None]), 0.0)
    keep_old = jnp.exp(old_max - new_max)
    old_sum = lax.dynamic_slice_in_dim(run_sum, row_start, TILE, 1)
    new_sum = old_sum * keep_old + jnp.sum(probs, axis=2)
    rounded = probs.astype(jnp.bfloat16)
    block_vals = lax.dynamic_slice_in_dim(src_values, col_start, TILE, 0).reshape(
        TILE, HEADS, HEAD_DIM
    )
    message = jnp.einsum("hij,jhc->ihc", rounded, block_vals, preferred_element_type=jnp.float32)
    old_acc = lax.dynamic_slice_in_dim(run_acc, row_start, TILE, 0).reshape(TILE, HEADS, HEAD_DIM)
    new_acc = (old_acc * keep_old.T[:, :, None] + message).reshape(TILE, HEADS * HEAD_DIM)
    run_max = lax.dynamic_update_slice_in_dim(run_max, new_max, row_start, 1)
    run_sum = lax.dynamic_update_slice_in_dim(run_sum, new_sum, row_start, 1)
    run_acc = lax.dynamic_update_slice_in_dim(run_acc, new_acc, row_start, 0)
    return (run_max, run_sum, run_acc)


def finish(row_top, row_sums, row_acc, self_logit, own_values, bias):
    last_max = jnp.maximum(row_top, self_logit)
    keep_old = jnp.exp(row_top - last_max)
    keep_self = jnp.exp(self_logit - last_max)
    denominator = row_sums * keep_old + keep_self
    row_count = row_acc.shape[0]
    own_wide = own_values.astype(jnp.float32).reshape(row_count, HEADS, HEAD_DIM)
    combined = (
        row_acc.reshape(row_count, HEADS, HEAD_DIM) * keep_old[:, :, None]
        + keep_self[:, :, None] * own_wide
    )
    mixed = (combined / denominator[:, :, None]).reshape(row_count, HEADS * HEAD_DIM)
    return jax.nn.elu(mixed + bias[None])


def local(
    src_feat, dst_feat, weight, att_src, att_dst, bias, tile_rows, tile_cols, tile_masks, tile_count
):
    src_values = project_rows(src_feat, weight)
    src_scores = head_scores(src_values, att_src).T
    own_values = project_rows(dst_feat, weight)
    dst_own = head_scores(own_values, att_dst)
    dst_cross = head_scores(own_values, att_src)
    dst_scores = lax.all_gather(dst_own.T, "col", axis=1, tiled=True)
    dest_rows = dst_scores.shape[1]
    run_max = jnp.full((HEADS, dest_rows), NEG_FILL, jnp.float32)
    run_sum = jnp.zeros((HEADS, dest_rows), jnp.float32)
    run_acc = jnp.zeros((dest_rows, HEADS * HEAD_DIM), jnp.float32)

    def one_tile(tile_slot, carry_state):
        row_start = tile_rows[0, 0, tile_slot] * TILE
        col_start = tile_cols[0, 0, tile_slot] * TILE
        return tile_update(
            carry_state,
            dst_scores,
            src_scores,
            src_values,
            tile_masks[0, 0, tile_slot],
            row_start,
            col_start,
        )

    run_max, run_sum, run_acc = lax.fori_loop(
        0, tile_count[0, 0], one_tile, (run_max, run_sum, run_acc)
    )
    global_top = lax.pmax(run_max, "col")
    factors = jnp.exp(run_max - global_top)
    scaled = (run_acc.reshape(dest_rows, HEADS, HEAD_DIM) * factors.T[:, :, None]).reshape(
        dest_rows, HEADS * HEAD_DIM
    )
    row_acc, row_sums = (
        lax.psum_scatter(scaled, "col", scatter_dimension=0, tiled=True),
        lax.psum_scatter((run_sum * factors).T, "col", scatter_dimension=0, tiled=True),
    )
    own_rows = row_acc.shape[0]
    row_top = lax.dynamic_slice_in_dim(global_top.T, lax.axis_index("col") * own_rows, own_rows, 0)
    self_logit = leaky_relu(dst_own + dst_cross)
    return finish(row_top, row_sums, row_acc, self_logit, own_values, bias)


def solution(mesh):
    placed = (
        P("col", None),
        P(("row", "col"), None),
        P(),
        P(),
        P(),
        P(),
        P("row", "col", None),
        P("row", "col", None),
        P("row", "col", None, None, None),
        P("row", "col"),
    )
    return jax.shard_map(
        local, mesh=mesh, in_specs=placed, out_specs=P(("row", "col"), None), check_vma=False
    )
```

profile of v0, /device:TPU:7, one launch (start us, length us, event | category | flops | bytes accessed | tf_op | source)
XLA Modules:
  0.0 2358.9 jit_solution(10622549759398922121)
XLA Ops:
  6.5 1.1 convolution_convert_fusion.1
  8.8 45.5 %all-gather = f32[32,64,8]{1,2,0:T(8,128)S(1)} all-gather(f32[1,64,8]{1,2,0:T(8,128)S(1)} %copy.37), channel_id=1, replica_groups=mesh['row'=8,'col'=32] {'col'}, dimensions={0}, use_global_device_ids=true | all-gather | bytes 67584 | tf_op jit(solution)/shard_map/all_gather | solution.py:78
  54.4 4.1 convolution_convert_fusion
  58.5 7.1 copy.39
  65.6 4.7 multiply_reduce_fusion
  70.3 2.5 broadcast_in_dim.42.clone
  72.8 909.2 %while.14 = (s32[]{:T(128)}, f32[8,2048]{1,0:T(8,128)S(1)}, f32[8,2048]{1,0:T(8,128)S(1)}, f32[2048,512]{1,0:T(8,128)}, s32[]{:T(128)}, /*index=5*/s32[1,1,160]{...) while((s32[]{:T(128)}, f32[8,2048]{1,0:T(8,128)S(1)}, ...), condition=%wide.region_5.6_spmd, body=%wide.region_2.5_spmd.sunk | while | flops 19811340 | bytes 3510579 | solution.py:97
  79.7 1.0 constant_dynamic-slice_fusion.11
  90.6 1.0 constant_dynamic-slice_fusion.11
  101.5 1.0 constant_dynamic-slice_fusion.11
  112.5 1.0 constant_dynamic-slice_fusion.11
  123.4 1.0 constant_dynamic-slice_fusion.11
  134.4 1.0 constant_dynamic-slice_fusion.11
  145.3 1.0 constant_dynamic-slice_fusion.11
  156.3 1.0 constant_dynamic-slice_fusion.11
  167.2 1.0 constant_dynamic-slice_fusion.11
  178.2 1.0 constant_dynamic-slice_fusion.11
  189.1 1.0 constant_dynamic-slice_fusion.11
  200.1 1.0 constant_dynamic-slice_fusion.11
  211.0 1.0 constant_dynamic-slice_fusion.11
  222.0 1.0 constant_dynamic-slice_fusion.11
  232.9 1.0 constant_dynamic-slice_fusion.11
  243.9 1.0 constant_dynamic-slice_fusion.11
  254.8 1.0 constant_dynamic-slice_fusion.11
  265.8 1.0 constant_dynamic-slice_fusion.11
  276.7 1.0 constant_dynamic-slice_fusion.11
  287.7 1.0 constant_dynamic-slice_fusion.11
  298.6 1.0 constant_dynamic-slice_fusion.11
  309.6 1.0 constant_dynamic-slice_fusion.11
  320.5 1.0 constant_dynamic-slice_fusion.11
  331.4 1.0 constant_dynamic-slice_fusion.11
  342.4 1.0 constant_dynamic-slice_fusion.11
  353.3 1.0 constant_dynamic-slice_fusion.11
  364.3 1.0 constant_dynamic-slice_fusion.11
  375.2 1.0 constant_dynamic-slice_fusion.11
  386.2 1.0 constant_dynamic-slice_fusion.11
  397.1 1.0 constant_dynamic-slice_fusion.11
  408.0 1.0 constant_dynamic-slice_fusion.11
  419.0 1.0 constant_dynamic-slice_fusion.11
  429.9 1.0 constant_dynamic-slice_fusion.11
  440.9 1.0 constant_dynamic-slice_fusion.11
  451.8 1.0 constant_dynamic-slice_fusion.11
  462.8 1.0 constant_dynamic-slice_fusion.11
  473.7 1.0 constant_dynamic-slice_fusion.11
  484.7 1.0 constant_dynamic-slice_fusion.11
  495.6 1.0 constant_dynamic-slice_fusion.11
  506.5 1.0 constant_dynamic-slice_fusion.11
  637.9 1.0 constant_dynamic-slice_fusion.11
  670.8 1.0 constant_dynamic-slice_fusion.11
  725.5 1.0 constant_dynamic-slice_fusion.11
  736.4 1.0 constant_dynamic-slice_fusion.11
  823.9 1.0 constant_dynamic-slice_fusion.11
  834.9 1.0 constant_dynamic-slice_fusion.11
  856.8 1.0 constant_dynamic-slice_fusion.11
  889.6 1.0 constant_dynamic-slice_fusion.11
  977.2 1.0 constant_dynamic-slice_fusion.11
  982.7 1075.6 %all-reduce.2.cloned.1.call-done = f32[8,2048]{1,0:T(8,128)} async-done(((f32[8,2048]{1,0:T(8,128)}), f32[8,2048]{1,0:T(8,128)}) %all-reduce.2.cloned.1.call-update) | async-done | bytes 65552 | tf_op jit(solution)/shard_map/pmax | solution.py:100
  2059.2 1.4 copy.48
  2060.6 2.5 mul.102
  2063.1 5.3 copy.42
  2068.4 6.5 mul.104
  2075.1 126.0 %reduce-scatter.7.cloned.1.call-done = f32[64,8]{1,0:T(8,128)} async-done(((f32[2048,8]{1,0:T(8,128)}), f32[64,8]{1,0:T(8,128)}) %reduce-scatter.7.cloned.1.call-update) | async-done | bytes 2064
  2203.7 147.1 %reduce-scatter.5.cloned.1.call-done = f32[64,512]{1,0:T(8,128)} async-done(((f32[2048,512]{1,0:T(8,128)}), f32[64,512]{1,0:T(8,128)}) %reduce-scatter.5.cloned.1.call-update) | async-done | bytes 131088 | tf_op jit(solution)/shard_map/reduce_scatter | solution.py:106
  2350.8 1.7 compare_select_fusion.1
  (1235 shorter events, 497.1 us)
Async XLA Ops:
  6.5 47.9 %copy-start = (bf16[4096,128]{1,0:T(8,128)(2,1)S(1)}, bf16[4096,128]{1,0:T(8,128)(2,1)}, u32[]{:S(2)}) copy-start(bf16[4096,128]{1,0:T(8,128)(2,1)} %param.12) | copy-start | bytes 3145732
  6.5 2051.7 %all-reduce.2.cloned.1.call-start = ((), (), s32[]{:S(2)}) async-start(), calls=%async_computation.2 | async-start | bytes 131072 | tf_op jit(solution)/shard_map/pmax | solution.py:100
  58.5 7.1 copy-start.2
  70.3 2.5 copy-start.4
  70.3 2.5 copy-start.5
  982.0 0.6 copy-start.1
  982.6 1218.5 %reduce-scatter.7.cloned.1.call-start = ((), (), s32[]{:S(2)}) async-start(), calls=%async_computation.4 | async-start | bytes 1081344
  2060.6 290.2 %reduce-scatter.5.cloned.1.call-start = ((), (), s32[]{:S(2)}) async-start(), calls=%async_computation.3 | async-start | bytes 4325376 | tf_op jit(solution)/shard_map/reduce_scatter | solution.py:106
  2074.9 275.9 %copy-start.3 = (f32[512]{0:T(512)S(1)}, f32[512]{0:T(512)}, u32[]{:S(2)}) copy-start(f32[512]{0:T(512)} %param.17) | copy-start | bytes 6148
Sparse Core Ops, SparseCore 0:
  982.8 1075.4 all-reduce.1
  2060.9 140.1 reduce-scatter.6
  2203.6 147.0 reduce-scatter.4
where the time goes:
time: 2390 us; the launch traced here: 2360 us
  waiting for transfers between devices  1350 us (56%)
  loops' own time  370 us (15%)
  local copies, waits for them, and re-layouts  271 us (11%)
  other arithmetic  264 us (11%)
  matrix products  46.8 us (2%)
  blocking collectives  45.5 us (2%)
    pmax x1, waiting for transfers between devices, local(): global_top = lax.pmax(run_max, 'col')  1080 us
    another operation x1, loops' own time, local(): lax.fori_loop(0, tile_count[0, 0], one_tile, (run_max, run_sum, run_acc))  370 us
    reduce_scatter x1, waiting for transfers between devices, local(): lax.psum_scatter(scaled, 'col', scatter_dimension=0, tiled=True)  147 us
    unnamed x4, waiting for transfers between devices  126 us
    dynamic_slice x166, local copies, waits for them, and re-layouts, tile_update(): lax.dynamic_slice_in_dim(run_acc, row_start, TILE, 0)  91 us
    dynamic_slice x166, local copies, waits for them, and re-layouts, tile_update(): lax.dynamic_slice_in_dim(src_values, col_start, TILE, 0)  86.1 us
    dynamic_update_slice x166, local copies, waits for them, and re-layouts, tile_update(): run_acc = lax.dynamic_update_slice_in_dim(run_acc, new_acc, row_start, 0)  71.4 us
    gt x83, other arithmetic, tile_update(): present = tile_mask[None] > 0  71.1 us
  transfers between devices with their start and end apart: 3, of which 3 were waited for; matrix products, arithmetic and copies ran while one was open for 1% of the time, Pallas kernels for 0%

commit v1 on v0

v1 whole, which is shorter than its diff:
```python
import functools

import jax
import jax.numpy as jnp
from jax import lax
from jax.experimental import pallas as pl
from jax.experimental.pallas import tpu as pltpu
from jax.sharding import PartitionSpec as P

HEADS = 8
HEAD_DIM = 64
TILE = 128
FEAT = HEADS * HEAD_DIM
NEG = -1e30
SPAN = 50.0
HALF = FEAT // 2
HALF_HEADS = HEADS // 2
BLOCK = HALF + 16
AUG = HEAD_DIM + 16
RING = 12
ORDER = 256

f32 = jnp.float32
bf16 = jnp.bfloat16


def leaky_relu(values):
    return jnp.maximum(values, 0.2 * values)


def split3(values):
    high = values.astype(bf16)
    rest = values - high.astype(f32)
    middle = rest.astype(bf16)
    low = (rest - middle.astype(f32)).astype(bf16)
    return high, middle, low


def transposed_dot(left, right):
    return lax.dot_general(left, right, (((0,), (0,)), ((), ())), preferred_element_type=f32)


def project_t(weight, features):
    return lax.dot_general(weight, features, (((0,), (1,)), ((), ())), preferred_element_type=f32).astype(bf16)


def attention_column(attention):
    wide = jnp.concatenate([attention] * HEADS, axis=1)
    head = lax.broadcasted_iota(jnp.int32, wide.shape, 0)
    lane_head = lax.broadcasted_iota(jnp.int32, wide.shape, 1) // HEAD_DIM
    wide = jnp.where(head == lane_head, wide, 0.0)
    terms = jnp.concatenate([part.astype(f32) for part in split3(wide)], axis=0).astype(bf16)
    return transposed_dot(terms, jnp.ones((terms.shape[0], 128), bf16))


def head_rows(values, column):
    product = values * column
    return [
        jnp.sum(product[h * HEAD_DIM : (h + 1) * HEAD_DIM], axis=0, keepdims=True) for h in range(HEADS)
    ]


def as_column(row, rows):
    return jnp.transpose(jnp.broadcast_to(row, (rows, row.shape[1])))


def scores_kernel(n_col, dst_ref, weight_ref, att_ref, rows_ref, cols_ref, count_ref,
                  score_ref, chip_ref, order_ref, pairs_ref, own, send_sem, recv_sem, feat_send, feat_recv):
    me = lax.axis_index("col")
    core = lax.rem(me, 2)
    partner = me + 1 - 2 * core
    barrier = pltpu.get_barrier_semaphore()

    def greet(step, carry):
        pl.semaphore_signal(barrier, inc=1, device_id={"col": lax.rem(me + step, n_col)},
                            device_id_type=pl.DeviceIdType.MESH)
        return carry

    lax.fori_loop(1, n_col, greet, 0)

    features = dst_ref[...]
    both = jnp.concatenate([features, features], axis=0)
    side = lax.broadcasted_iota(jnp.int32, both.shape, 0) // features.shape[0]
    both = jnp.where(side == core, both, jnp.zeros_like(both))
    values = project_t(weight_ref[...], both).astype(f32)
    own[...] = jnp.concatenate(head_rows(values, attention_column(att_ref[...])), axis=0)
    score_ref[me] = own[...]
    half = features.shape[0]
    chip_ref[pl.ds(pl.multiple_of(core * half, half), half), :] = features

    pl.semaphore_wait(barrier, n_col - 1)

    def score_copy(target, source_slot):
        return pltpu.make_async_remote_copy(
            src_ref=own, dst_ref=score_ref.at[me], send_sem=send_sem.at[target], recv_sem=recv_sem.at[source_slot],
            device_id={"col": target}, device_id_type=pl.DeviceIdType.MESH)

    def send(step, carry):
        score_copy(lax.rem(me + step, n_col), me).start()
        return carry

    lax.fori_loop(1, n_col, send, 0)
    feat_copy = pltpu.make_async_remote_copy(
        src_ref=dst_ref, dst_ref=chip_ref.at[pl.ds(pl.multiple_of(core * half, half), half), :],
        send_sem=feat_send, recv_sem=feat_recv, device_id={"col": partner}, device_id_type=pl.DeviceIdType.MESH)
    feat_copy.start()

    slots = rows_ref.shape[1]
    row_block = rows_ref[...].astype(f32)
    slot = lax.broadcasted_iota(jnp.int32, (1, slots), 1)
    row_block = jnp.where(slot < count_ref[...], row_block, 255.0)
    pad = jnp.full((1, ORDER - slots), 255.0, f32)
    row_block = jnp.concatenate([row_block, pad], axis=1)
    across = jnp.broadcast_to(row_block, (ORDER, ORDER))
    down = jnp.transpose(across)
    lane = lax.broadcasted_iota(jnp.int32, (ORDER, ORDER), 1)
    sub = lax.broadcasted_iota(jnp.int32, (ORDER, ORDER), 0)
    before = jnp.sum(jnp.where((down == across) & (sub < lane), 1.0, 0.0), axis=0, keepdims=True)
    block_id = lax.broadcasted_iota(jnp.int32, (16, ORDER), 0).astype(f32)
    counts = jnp.sum(jnp.where(block_id == row_block, 1.0, 0.0), axis=1, keepdims=True)
    pairs = jnp.floor((counts + 1.0) * 0.5)
    start = jnp.sum(jnp.where(block_id < row_block, pairs, 0.0), axis=0, keepdims=True)
    place = jnp.where(row_block < 254.0, 2.0 * start + before, -1.0)
    place_down = jnp.transpose(jnp.broadcast_to(place, (ORDER, ORDER)))
    columns = jnp.concatenate([cols_ref[...].astype(f32), jnp.zeros((1, ORDER - slots), f32)], axis=1)
    lane_row = lax.broadcasted_iota(jnp.int32, (1, ORDER), 1).astype(f32)
    code = 1.0 + lane_row + 256.0 * columns + 8192.0 * jnp.minimum(row_block, 15.0)
    code_down = jnp.transpose(jnp.broadcast_to(code, (ORDER, ORDER)))
    found = jnp.sum(jnp.where(place_down == lane.astype(f32), code_down, 0.0), axis=0, keepdims=True)
    order_ref[...] = found.astype(jnp.int32)
    pairs_ref[...] = jnp.broadcast_to(jnp.sum(pairs, axis=0, keepdims=True), (1, 128)).astype(jnp.int32)

    def finish(step, carry):
        peer = lax.rem(me + step, n_col)
        done = score_copy(peer, peer)
        done.wait_send()
        done.wait_recv()
        return carry

    lax.fori_loop(1, n_col, finish, 0)
    feat_copy.wait()


def edges_kernel(order_ref, pairs_ref, score_ref, feat_ref, weight_ref, att_ref, mask_hbm,
                 out_ref, scaled, ratio, ratio_dst, src_score, dst_score, acc, masks, mask_sem):
    n_blocks = acc.shape[0]
    n_cols = scaled.shape[0]
    total = pairs_ref[0, 0]

    def decode(position):
        code = order_ref[0, position]
        index = jnp.maximum(code - 1, 0)
        return code, index & 255, (index >> 8) & 31, index >> 13

    def mask_copy(pair, side, slot_at):
        ring = lax.rem(pair, RING)
        return pltpu.make_async_copy(mask_hbm.at[slot_at], masks.at[ring, side], mask_sem.at[ring, side])

    def fetch(pair):
        first = decode(2 * pair)
        second = decode(2 * pair + 1)
        mask_copy(pair, 0, first[1]).start()

        @pl.when(second[0] > 0)
        def _():
            mask_copy(pair, 1, second[1]).start()

        @pl.when(second[0] == 0)
        def _():
            masks[lax.rem(pair, RING), 1] = jnp.zeros((TILE, TILE), jnp.int32)

    def arrive(pair):
        mask_copy(pair, 0, 0).wait()

        @pl.when(decode(2 * pair + 1)[0] > 0)
        def _():
            mask_copy(pair, 1, 0).wait()

    def prefetch(pair, carry):
        @pl.when(pair < total)
        def _():
            fetch(pair)
        return carry

    lax.fori_loop(0, RING - 1, prefetch, 0)

    column = attention_column(att_ref[...])

    def source_block(block, carry):
        low, high = carry
        at = pl.multiple_of(block * TILE, TILE)
        values = project_t(weight_ref[...], feat_ref[pl.ds(at, TILE), :]).astype(f32)
        rows = head_rows(values, column)
        pad = jnp.zeros((14, TILE), f32)
        for h in range(HEADS):
            grow = jnp.exp(rows[h])
            fall = jnp.exp(-0.8 * rows[h])
            grow_high = grow.astype(bf16).astype(f32)
            scaled[block, h, 0:HEAD_DIM, :] = (values[h * HEAD_DIM : (h + 1) * HEAD_DIM] * grow).astype(bf16)
            scaled[block, h, HEAD_DIM:AUG, :] = jnp.concatenate([grow_high, grow - grow_high, pad], axis=0).astype(bf16)
            ratio[block, h] = jnp.broadcast_to(fall, (16, TILE)).astype(bf16)
        stacked = jnp.concatenate(rows, axis=0)
        src_score[block] = stacked
        return jnp.minimum(low, stacked), jnp.maximum(high, stacked)

    low, high = lax.fori_loop(0, n_cols, source_block,
                              (jnp.full((HEADS, TILE), 1e30, f32), jnp.full((HEADS, TILE), -1e30, f32)))

    spread_head = lax.broadcasted_iota(jnp.int32, (HEADS, HEADS * TILE), 0)
    spread_lane = lax.broadcasted_iota(jnp.int32, (HEADS, HEADS * TILE), 1) // TILE
    spread = jnp.where(spread_head == spread_lane, 1.0, 0.0).astype(bf16)

    def dst_block(block, carry):
        low, high = carry
        score = score_ref[2 * block] + score_ref[2 * block + 1]
        dst_score[block] = score
        fall = jnp.exp(-0.8 * score).astype(bf16)
        wide = transposed_dot(fall, spread).astype(bf16)
        for h in range(HEADS):
            ratio_dst[block, h] = wide[:, h * TILE : (h + 1) * TILE]
        acc[block] = jnp.zeros(acc.shape[1:], f32)
        return jnp.minimum(low, score), jnp.maximum(high, score)

    low, high = lax.fori_loop(0, n_blocks, dst_block, (low, high))
    factored = (jnp.max(high) <= SPAN) & (jnp.min(low) >= -SPAN)

    @pl.when(factored)
    def _():
        def pair_step(pair, carry):
            @pl.when(pair + RING - 1 < total)
            def _():
                fetch(pair + RING - 1)

            arrive(pair)
            _, _, col_a, block = decode(2 * pair)
            _, _, col_b, _ = decode(2 * pair + 1)
            ring = lax.rem(pair, RING)
            mask_a = masks[ring, 0].astype(f32).astype(bf16).reshape(8, 16, TILE)
            mask_b = masks[ring, 1].astype(f32).astype(bf16).reshape(8, 16, TILE)
            one = jnp.ones((), bf16)
            for h in range(HEADS):
                fall_dst = ratio_dst[block, h].reshape(8, 16, TILE)
                weight_a = jnp.maximum(fall_dst * ratio[col_a, h][None], one) * mask_a
                weight_b = jnp.maximum(fall_dst * ratio[col_b, h][None], one) * mask_b
                edge = jnp.concatenate([weight_a.reshape(TILE, TILE), weight_b.reshape(TILE, TILE)], axis=1)
                source = jnp.concatenate([scaled[col_a, h], scaled[col_b, h]], axis=1)
                acc[block, h] += lax.dot_general(source, edge, (((1,), (1,)), ((), ())), preferred_element_type=f32)
            return carry

        lax.fori_loop(0, total, pair_step, 0)

        def reference_rows(block, carry):
            for h in range(HEADS):
                acc[block, h, 66:67, :] = dst_score[block, h : h + 1, :]
            return carry

        lax.fori_loop(0, n_blocks, reference_rows, 0)

    @pl.when(jnp.logical_not(factored))
    def _():
        def empty_rows(block, carry):
            for h in range(HEADS):
                acc[block, h, 66:67, :] = jnp.full((1, TILE), NEG, f32)
            return carry

        lax.fori_loop(0, n_blocks, empty_rows, 0)

        def one_tile(ring, side, col, block):
            present = jnp.transpose(masks[ring, side].astype(f32)) > 0.0
            at = pl.multiple_of(col * TILE, TILE)
            masks_free = project_t(weight_ref[...], feat_ref[pl.ds(at, TILE), :])
            for h in range(HEADS):
                source = as_column(src_score[col, h : h + 1, :], TILE)
                logit = leaky_relu(source + dst_score[block, h : h + 1, :])
                logit = jnp.where(present, logit, NEG)
                old_max = acc[block, h, 66:67, :]
                new_max = jnp.maximum(old_max, jnp.max(logit, axis=0, keepdims=True))
                prob = jnp.where(present, jnp.exp(logit - new_max), 0.0)
                keep = jnp.exp(old_max - new_max)
                message = jnp.dot(masks_free[h * HEAD_DIM : (h + 1) * HEAD_DIM], prob.astype(bf16),
                                  preferred_element_type=f32)
                acc[block, h, 0:HEAD_DIM, :] = acc[block, h, 0:HEAD_DIM, :] * keep + message
                acc[block, h, 64:65, :] = acc[block, h, 64:65, :] * keep + jnp.sum(prob, axis=0, keepdims=True)
                acc[block, h, 66:67, :] = new_max

        def pair_step(pair, carry):
            @pl.when(pair + RING - 1 < total)
            def _():
                fetch(pair + RING - 1)

            arrive(pair)
            ring = lax.rem(pair, RING)
            for side in range(2):
                _, _, col, _ = decode(2 * pair + side)
                one_tile(ring, side, col, decode(2 * pair)[3])
            return carry

        lax.fori_loop(0, total, pair_step, 0)

    def store_block(block, carry):
        for half in range(2):
            logs = []
            for g in range(HALF_HEADS):
                h = half * HALF_HEADS + g
                denominator = acc[block, h, 64:65, :] + acc[block, h, 65:66, :]
                some = denominator > 0.0
                safe = jnp.where(some, denominator, 1.0)
                out_ref[half, block, g * HEAD_DIM : (g + 1) * HEAD_DIM, :] = (
                    acc[block, h, 0:HEAD_DIM, :] * (1.0 / safe)).astype(bf16)
                logs.append(jnp.where(some, acc[block, h, 66:67, :] + jnp.log(safe), NEG))
            out_ref[half, block, HALF:BLOCK, :] = pack_logs(jnp.concatenate(logs, axis=0))
        return carry

    lax.fori_loop(0, n_blocks, store_block, 0)


def pack_logs(logs):
    high, middle, low = [part.astype(f32) for part in split3(logs)]
    return jnp.concatenate([high, middle, low, jnp.zeros_like(high)], axis=0).astype(bf16)


def unpack_logs(rows):
    wide = rows.astype(f32)
    n = HALF_HEADS
    return wide[0:n] + wide[n : 2 * n] + wide[2 * n : 3 * n]


def merge_blocks(blocks):
    logs = [unpack_logs(block[HALF:BLOCK]) for block in blocks]
    top = functools.reduce(jnp.maximum, logs)
    grow = [jnp.exp(log - top) for log in logs]
    total = functools.reduce(jnp.add, grow)
    share = [g * (1.0 / total) for g in grow]
    parts = []
    for h in range(HALF_HEADS):
        at = slice(h * HEAD_DIM, (h + 1) * HEAD_DIM)
        terms = [block[at].astype(f32) * s[h : h + 1] for block, s in zip(blocks, share)]
        parts.append(functools.reduce(jnp.add, terms).astype(bf16))
    return parts, pack_logs(top + jnp.log(total))


def store_block_parts(ref, index, merged):
    parts, logs = merged
    for h, part in enumerate(parts):
        ref[index + (slice(h * HEAD_DIM, (h + 1) * HEAD_DIM), slice(None))] = part
    ref[index + (slice(HALF, BLOCK), slice(None))] = logs


def merge_kernel(n_y, n_z, part_ref, chip_ref, weight_ref, att_src_ref, att_dst_ref, bias_ref, out_ref,
                 own, pair_in, summed, y_in, z_sum, z_in, self_values, self_logit, fin, fin_in,
                 own_sem, pair_send, pair_recv, y_send, y_recv, z_send, z_recv, fin_send, fin_recv):
    me = lax.axis_index("col")
    core = lax.rem(me, 2)
    chip = me // 2
    y = lax.rem(chip, n_y)
    z = chip // n_y
    partner = me + 1 - 2 * core

    def at(z_at, y_at):
        return {"col": (z_at * n_y + y_at) * 2 + core}

    mesh_id = pl.DeviceIdType.MESH
    barrier = pltpu.get_barrier_semaphore()
    pl.semaphore_signal(barrier, inc=1, device_id={"col": partner}, device_id_type=mesh_id)
    for step in range(1, n_y):
        pl.semaphore_signal(barrier, inc=1, device_id=at(z, lax.rem(y + step, n_y)), device_id_type=mesh_id)
    for step in range(1, n_z):
        pl.semaphore_signal(barrier, inc=1, device_id=at(lax.rem(z + step, n_z), y), device_id_type=mesh_id)

    def z_of(step):
        return lax.rem(z + 1 + step, n_z)

    def own_copy(step):
        rows = pl.ds(z_of(step) * n_y, n_y)
        return pltpu.make_async_copy(part_ref.at[core, rows], own.at[rows], own_sem.at[step])

    def pair_copy(step):
        rows = pl.ds(z_of(step) * n_y, n_y)
        return pltpu.make_async_remote_copy(
            src_ref=part_ref.at[1 - core, rows], dst_ref=pair_in.at[rows], send_sem=pair_send.at[step],
            recv_sem=pair_recv.at[step], device_id={"col": partner}, device_id_type=mesh_id)

    def y_copy(step, dy):
        block = z_of(step) * n_y + lax.rem(y + dy, n_y)
        return pltpu.make_async_remote_copy(
            src_ref=summed.at[block], dst_ref=y_in.at[step, dy - 1], send_sem=y_send.at[step, dy - 1],
            recv_sem=y_recv.at[step, dy - 1], device_id=at(z, lax.rem(y + dy, n_y)), device_id_type=mesh_id)

    def z_copy(step):
        return pltpu.make_async_remote_copy(
            src_ref=z_sum.at[step], dst_ref=z_in.at[step], send_sem=z_send.at[step],
            recv_sem=z_recv.at[step], device_id=at(z_of(step), y), device_id_type=mesh_id)

    for step in range(n_z):
        own_copy(step).start()

    values = project_t(weight_ref[...], chip_ref[...]).astype(f32)
    self_values[...] = values
    cross = jnp.concatenate(head_rows(values, attention_column(att_src_ref[...])), axis=0)
    direct = jnp.concatenate(head_rows(values, attention_column(att_dst_ref[...])), axis=0)
    logit = leaky_relu(cross + direct)
    self_logit[0] = logit
    self_logit[1] = jnp.concatenate([logit[HALF_HEADS:], logit[:HALF_HEADS]], axis=0)

    pl.semaphore_wait(barrier, 1 + (n_y - 1) + (n_z - 1))
    for step in range(n_z):
        pair_copy(step).start()

    def pair_merge(step):
        own_copy(step).wait()
        pair_copy(step).wait()
        for dy in range(n_y):
            block = z_of(step) * n_y + lax.rem(y + dy, n_y)
            store_block_parts(summed, (block,), merge_blocks([own[block], pair_in[block]]))
        for dy in range(1, n_y):
            y_copy(step, dy).start()

    def y_merge(step):
        for dy in range(1, n_y):
            y_copy(step, dy).wait()
        blocks = [summed[z_of(step) * n_y + y]] + [y_in[step, dy - 1] for dy in range(1, n_y)]
        store_block_parts(z_sum, (step,), merge_blocks(blocks))
        if step < n_z - 1:
            z_copy(step).start()

    for step in range(n_z):
        pair_merge(step)
        if step > 0:
            y_merge(step - 1)
    y_merge(n_z - 1)
    for step in range(n_z - 1):
        z_copy(step).wait()

    blocks = [z_sum[n_z - 1]] + [z_in[step] for step in range(n_z - 1)]
    logs = [unpack_logs(block[HALF:BLOCK]) for block in blocks] + [self_logit[core][0:HALF_HEADS]]
    top = functools.reduce(jnp.maximum, logs)
    grow = [jnp.exp(log - top) for log in logs]
    inverse = 1.0 / functools.reduce(jnp.add, grow)
    pieces = []
    for h in range(HALF_HEADS):
        rows = slice(h * HEAD_DIM, (h + 1) * HEAD_DIM)
        start = pl.multiple_of(core * HALF, HALF) + h * HEAD_DIM
        terms = [block[rows].astype(f32) * g[h : h + 1] for block, g in zip(blocks, grow)]
        terms.append(self_values[pl.ds(start, HEAD_DIM), :] * grow[-1][h : h + 1])
        pieces.append(functools.reduce(jnp.add, terms) * inverse[h : h + 1])
    mixed = jnp.transpose(jnp.concatenate(pieces, axis=0))
    bias = jnp.where(core == 0, bias_ref[:, 0:HALF], bias_ref[:, HALF:FEAT])
    mixed = mixed + bias
    fin[...] = jnp.where(mixed > 0, mixed, jnp.exp(jnp.minimum(mixed, 0.0)) - 1.0)
    half = out_ref.shape[0]
    final = pltpu.make_async_remote_copy(
        src_ref=fin.at[pl.ds(pl.multiple_of((1 - core) * half, half), half), :], dst_ref=fin_in,
        send_sem=fin_send, recv_sem=fin_recv, device_id={"col": partner}, device_id_type=mesh_id)
    final.start()
    mine = fin[pl.ds(pl.multiple_of(core * half, half), half), :]
    final.wait()
    theirs = fin_in[...]
    out_ref[:, 0:HALF] = jnp.where(core == 0, mine, theirs)
    out_ref[:, HALF:FEAT] = jnp.where(core == 0, theirs, mine)


VMEM = pl.BlockSpec(memory_space=pltpu.VMEM)
SMEM = pl.BlockSpec(memory_space=pltpu.SMEM)
ANY = pl.BlockSpec(memory_space=pl.ANY)
DMA = pltpu.SemaphoreType.DMA


def destination_scores(n_col, dst_feat, weight, att_dst, tile_rows, tile_cols, tile_count):
    own = dst_feat.shape[0]
    return pl.pallas_call(
        functools.partial(scores_kernel, n_col),
        name="destination_scores",
        out_shape=(
            jax.ShapeDtypeStruct((n_col, HEADS, 2 * own), f32),
            jax.ShapeDtypeStruct((2 * own, dst_feat.shape[1]), bf16),
            jax.ShapeDtypeStruct((1, ORDER), jnp.int32),
            jax.ShapeDtypeStruct((1, 128), jnp.int32),
        ),
        in_specs=[VMEM] * 6,
        out_specs=(VMEM,) * 4,
        scratch_shapes=[pltpu.VMEM((HEADS, 2 * own), f32), DMA((n_col,)), DMA((n_col,)), DMA(()), DMA(())],
        compiler_params=pltpu.CompilerParams(collective_id=0, has_side_effects=True,
                                             vmem_limit_bytes=16 * 1024 * 1024),
    )(dst_feat, weight, att_dst, tile_rows, tile_cols, tile_count)


def edge_sums(order, pairs, scores, src_feat, weight, att_src, masks):
    n_cols = src_feat.shape[0] // TILE
    n_blocks = scores.shape[0] // 2
    return pl.pallas_call(
        edges_kernel,
        name="edge_sums",
        out_shape=jax.ShapeDtypeStruct((2, n_blocks, BLOCK, TILE), bf16),
        in_specs=[SMEM, SMEM, VMEM, VMEM, VMEM, VMEM, ANY],
        out_specs=VMEM,
        scratch_shapes=[
            pltpu.VMEM((n_cols, HEADS, AUG, TILE), bf16),
            pltpu.VMEM((n_cols, HEADS, 16, TILE), bf16),
            pltpu.VMEM((n_blocks, HEADS, TILE, TILE), bf16),
            pltpu.VMEM((n_cols, HEADS, TILE), f32),
            pltpu.VMEM((n_blocks, HEADS, TILE), f32),
            pltpu.VMEM((n_blocks, HEADS, AUG, TILE), f32),
            pltpu.VMEM((RING, 2, TILE, TILE), jnp.int32),
            DMA((RING, 2)),
        ],
        compiler_params=pltpu.CompilerParams(vmem_limit_bytes=48 * 1024 * 1024),
    )(order, pairs, scores, src_feat, weight, att_src, masks)


def merge(n_y, n_z, parts, chip_feat, weight, att_src, att_dst, bias):
    n_blocks = n_y * n_z
    own = chip_feat.shape[0] // 2
    return pl.pallas_call(
        functools.partial(merge_kernel, n_y, n_z),
        name="merge",
        out_shape=jax.ShapeDtypeStruct((own, FEAT), f32),
        in_specs=[ANY, VMEM, VMEM, VMEM, VMEM, VMEM],
        out_specs=VMEM,
        scratch_shapes=[
            pltpu.VMEM((n_blocks, BLOCK, TILE), bf16),
            pltpu.VMEM((n_blocks, BLOCK, TILE), bf16),
            pltpu.VMEM((n_blocks, BLOCK, TILE), bf16),
            pltpu.VMEM((n_z, n_y - 1, BLOCK, TILE), bf16),
            pltpu.VMEM((n_z, BLOCK, TILE), bf16),
            pltpu.VMEM((n_z - 1, BLOCK, TILE), bf16),
            pltpu.VMEM((FEAT, TILE), f32),
            pltpu.VMEM((2, HEADS, TILE), f32),
            pltpu.VMEM((TILE, HALF), f32),
            pltpu.VMEM((own, HALF), f32),
            DMA((n_z,)), DMA((n_z,)), DMA((n_z,)), DMA((n_z, n_y - 1)), DMA((n_z, n_y - 1)),
            DMA((n_z - 1,)), DMA((n_z - 1,)), DMA(()), DMA(()),
        ],
        compiler_params=pltpu.CompilerParams(collective_id=1, has_side_effects=True,
                                             vmem_limit_bytes=32 * 1024 * 1024),
    )(parts, chip_feat, weight, att_src, att_dst, bias)


def local(n_col, src_feat, dst_feat, weight, att_src, att_dst, bias, tile_rows, tile_cols, tile_masks, tile_count):
    slots = tile_rows.shape[2]
    scores, chip_feat, order, pairs = destination_scores(
        n_col, dst_feat, weight, att_dst, tile_rows.reshape(1, slots), tile_cols.reshape(1, slots), tile_count)
    parts = edge_sums(order, pairs, scores, src_feat, weight, att_src, tile_masks.reshape(slots, TILE, TILE))
    n_y = 4
    return merge(n_y, n_col // (2 * n_y), parts, chip_feat, weight, att_src, att_dst, bias.reshape(1, FEAT))


def solution(mesh):
    placed = (
        P("col", None),
        P(("row", "col"), None),
        P(),
        P(),
        P(),
        P(),
        P("row", "col", None),
        P("row", "col", None),
        P("row", "col", None, None, None),
        P("row", "col"),
    )
    return jax.shard_map(
        functools.partial(local, mesh.shape["col"]), mesh=mesh, in_specs=placed,
        out_specs=P(("row", "col"), None), check_vma=False,
    )
```

time: 2390 us -> 125 us (0.05); the launches traced: 2360 us -> 124 us
  waiting for transfers between devices: 1350 us -> 0 us
  loops' own time: 370 us -> 0 us
  other arithmetic: 264 us -> 0 us
  local copies, waits for them, and re-layouts: 271 us -> 7.13 us
  Pallas kernels: 0 us -> 116 us
  matrix products: 46.8 us -> 0 us
  blocking collectives: 45.5 us -> 0 us
    pmax x1 -> x0, waiting for transfers between devices: 1080 us -> none  [local(): global_top = lax.pmax(run_max, 'col')]
    another operation x1 -> x0, loops' own time: 370 us -> none  [local(): lax.fori_loop(0, tile_count[0, 0], one_tile, (run_max, run_sum, run_acc))]
    dynamic_slice x415 -> x0, local copies, waits for them, and re-layouts: 178 us -> none  [the longest x166 91 us: tile_update(): lax.dynamic_slice_in_dim(run_acc, row_start, TILE, 0)]
    reduce_scatter x1 -> x0, waiting for transfers between devices: 147 us -> none  [local(): lax.psum_scatter(scaled, 'col', scatter_dimension=0, tiled=True)]
    unnamed x4 -> x0, waiting for transfers between devices: 126 us -> none
    pallas_call x0 -> x3, Pallas kernels: none -> 116 us  [the longest x1 64.2 us: edge_sums(): pl.pallas_call(edges_kernel, name='edge_sums', out_shape=jax.ShapeDtypeSt...]
    mul x167 -> x0, other arithmetic: 105 us -> none  [the longest x83 49.5 us: one_tile(): col_start = tile_cols[0, 0, tile_slot] * TILE]
    dynamic_update_slice x166 -> x0, local copies, waits for them, and re-layouts: 71.4 us -> none  [tile_update(): run_acc = lax.dynamic_update_slice_in_dim(run_acc, new_acc, row_start, 0)]
  transfers between devices with their start and end apart: 3 -> 0, of which waited for: 3 -> 0; matrix products, arithmetic and copies ran while one was open for 1% -> 0% of each run, Pallas kernels for 0% -> 0%
where the time goes in v1:
time: 125 us; the launch traced here: 124 us
  Pallas kernels  116 us (93%)
  local copies, waits for them, and re-layouts  7.13 us (6%)
    pallas_call x1, Pallas kernels, edge_sums(): pl.pallas_call(edges_kernel, name='edge_sums', out_shape=jax.ShapeDtypeSt...  64.2 us
    pallas_call x1, Pallas kernels, merge(): pl.pallas_call(functools.partial(merge_kernel, n_y, n_z), name='merge', o...  40.2 us
    pallas_call x1, Pallas kernels, destination_scores(): pl.pallas_call(functools.partial(scores_kernel, n_col), name='destination...  12.1 us
    unnamed x21, local copies, waits for them, and re-layouts  7.13 us

profile of v1, /device:TPU:7, one launch (start us, length us, event | category | flops | bytes accessed | tf_op | source)
XLA Modules:
  0.0 124.4 jit_solution(1004595839650922034)
XLA Ops:
  0.0 0.0 copy-start.5
  0.0 0.0 copy-start.7
  0.7 0.0 copy-start
  0.7 0.9 copy-done
  1.6 0.0 copy-start.4
  1.6 0.7 copy-done.4
  2.3 0.0 copy-start.6
  2.3 0.7 copy-done.6
  3.0 0.0 copy-start.8
  3.0 0.7 copy-done.8
  3.7 0.0 copy-start.9
  3.7 0.7 copy-done.9
  4.4 12.1 %destination_scores.1 = (f32[32,8,128]{2,1,0:T(8,128)S(1)}, bf16[128,128]{1,0:T(8,128)(2,1)S(1)}, s32[1,256]{1,0:T(1,128)S(1)}, s32[1,128]{1,0:T(1,128)S(1)}) custom-call(bf16[64,128]{1,0:T(8,128)(2,1)S(1)} %copy-done.6, bf16[128,512]{1,0:T(8,128)(2,1)S(1)} %copy-done, f32[8,64]{1,0:T(8,128)S(1)} %copy-done.4, s32[1,160]{1,0:T(1,128)S(1)} %bitcast.5, ...), custom_call_target="tpu_custom_call" | custom-call | tf_op jit(solution)/shard_map/destination_scores/pallas_call | solution.py:470
  16.5 0.0 copy-start.1
  16.5 0.9 copy-done.1
  17.4 0.0 copy-start.2
  17.4 1.2 copy-done.2
  18.6 0.0 copy-start.3
  18.6 0.7 copy-done.3
  19.3 64.2 %edge_sums.1.part_ref = bf16[2,16,272,128]{3,2,1,0:T(8,128)(2,1)S(1)} custom-call(s32[1,256]{1,0:T(1,128)S(1)} %get-tuple-element.9.order_ref, s32[1,128]{1,0:T(1,128)S(1)} %get-tuple-element.10.pairs_ref, f32[32,8,128]{2,1,0:T(8,128)S(1)} %get-tuple-element.11.score_ref, bf16[4096,128]{1,0:T(8,128)(2,1)S(1)} %copy-done.2, bf16[128,512]{1,0:T(8,128)(2,1)S(1)} %copy-done.1, ...), custom_call_target="tpu_custom_call" | custom-call | tf_op jit(solution)/shard_map/edge_sums/pallas_call | solution.py:490
  83.5 0.0 copy-done.5
  83.5 0.0 copy-done.7
  83.5 40.2 %merge.1 = f32[64,512]{1,0:T(8,128)S(1)} custom-call(bf16[2,16,272,128]{3,2,1,0:T(8,128)(2,1)S(1)} %edge_sums.1.part_ref, bf16[128,128]{1,0:T(8,128)(2,1)S(1)} %get-tuple-element.12.chip_ref, bf16[128,512]{1,0:T(8,128)(2,1)S(1)} %copy-done.1, f32[8,64]{1,0:T(8,128)S(1)} %copy-done.3, f32[8,64]{1,0:T(8,128)S(1)} %copy-done.5, f32[1,512]{1,0:T(1,128)S(1)} %bitcast.4), custom_call_target="tpu_custom_call" | custom-call | tf_op jit(solution)/shard_map/merge/pallas_call | solution.py:513
  123.7 0.7 copy.13
Async XLA Ops:
  0.0 83.5 %copy-start.5 = (f32[8,64]{1,0:T(8,128)S(1)}, f32[8,64]{1,0:T(8,128)}, u32[]{:S(2)}) copy-start(f32[8,64]{1,0:T(8,128)} %att_dst_ref.1) | copy-start | bytes 6148
  0.0 83.5 %copy-start.7 = (f32[512]{0:T(512)S(1)}, f32[512]{0:T(512)}, u32[]{:S(2)}) copy-start(f32[512]{0:T(512)} %param.15) | copy-start | bytes 6148
  0.7 0.9 copy-start
  1.6 0.7 copy-start.4
  2.3 0.7 copy-start.6
  3.0 0.7 copy-start.8
  3.7 0.7 copy-start.9
  16.5 0.9 copy-start.1
  17.4 1.2 copy-start.2
  18.6 0.7 copy-start.3

commit v2 on v1

v2 whole, which is shorter than its diff:
```python
import functools

import jax
import jax.numpy as jnp
from jax import lax
from jax.experimental import pallas as pl
from jax.experimental.pallas import tpu as pltpu
from jax.sharding import PartitionSpec as P

HEADS = 8
HEAD_DIM = 64
TILE = 128
FEAT = HEADS * HEAD_DIM
NEG = -1e30
SPAN = 50.0
HALF = FEAT // 2
HALF_HEADS = HEADS // 2
BLOCK = HALF + 16
AUG = HEAD_DIM + 16
GROUP = 4
RING = 16
ORDER = 256

f32 = jnp.float32
bf16 = jnp.bfloat16


def leaky_relu(values):
    return jnp.maximum(values, 0.2 * values)


def split3(values):
    high = values.astype(bf16)
    rest = values - high.astype(f32)
    middle = rest.astype(bf16)
    low = (rest - middle.astype(f32)).astype(bf16)
    return high, middle, low


def transposed_dot(left, right):
    return lax.dot_general(left, right, (((0,), (0,)), ((), ())), preferred_element_type=f32)


def project_t(weight, features):
    return lax.dot_general(weight, features, (((0,), (1,)), ((), ())), preferred_element_type=f32).astype(bf16)


def project_rows_t(weight_t, features):
    return lax.dot_general(weight_t, features, (((1,), (1,)), ((), ())), preferred_element_type=f32).astype(bf16)


def attention_column(attention):
    wide = jnp.concatenate([attention] * HEADS, axis=1)
    head = lax.broadcasted_iota(jnp.int32, wide.shape, 0)
    lane_head = lax.broadcasted_iota(jnp.int32, wide.shape, 1) // HEAD_DIM
    wide = jnp.where(head == lane_head, wide, 0.0)
    terms = jnp.concatenate([part.astype(f32) for part in split3(wide)], axis=0).astype(bf16)
    return transposed_dot(terms, jnp.ones((terms.shape[0], 128), bf16))


def head_rows(values, column):
    product = values * column
    return [
        jnp.sum(product[h * HEAD_DIM : (h + 1) * HEAD_DIM], axis=0, keepdims=True) for h in range(HEADS)
    ]


def as_column(row, rows):
    return jnp.transpose(jnp.broadcast_to(row, (rows, row.shape[1])))


def scores_kernel(n_col, dst_hbm, weight_hbm, att_src_hbm, att_dst_hbm, rows_hbm, cols_hbm, count_hbm, feat_hbm,
                  score_ref, self_ref, cross_ref, order_ref, pairs_ref, scaled, ratio, src_score, range_ref,
                  dst_in, weight_in, att_src_in, att_dst_in, rows_in, cols_in, count_in, feat_in,
                  own, own_cross, own_self, weight_t, spread,
                  load_sem, send_sem, recv_sem, part_send, part_recv):
    me = lax.axis_index("col")
    core = lax.rem(me, 2)
    partner = me + 1 - 2 * core
    loads = [
        pltpu.make_async_copy(source, target, load_sem.at[i])
        for i, (source, target) in enumerate([
            (weight_hbm, weight_in), (dst_hbm, dst_in), (att_src_hbm, att_src_in), (att_dst_hbm, att_dst_in),
            (rows_hbm, rows_in), (cols_hbm, cols_in), (count_hbm, count_in), (feat_hbm, feat_in)])
    ]
    for load in loads:
        load.start()
    barrier = pltpu.get_barrier_semaphore()

    def greet(step, carry):
        pl.semaphore_signal(barrier, inc=1, device_id={"col": lax.rem(me + step, n_col)},
                            device_id_type=pl.DeviceIdType.MESH)
        return carry

    lax.fori_loop(1, n_col, greet, 0)
    for load in loads[:-1]:
        load.wait()

    weight_t[...] = jnp.transpose(weight_in[...])
    column = attention_column(att_src_in[...])
    features = dst_in[...]
    both = jnp.concatenate([features, features], axis=0)
    side = lax.broadcasted_iota(jnp.int32, both.shape, 0) // features.shape[0]
    both = jnp.where(side == core, both, jnp.zeros_like(both))
    values = project_rows_t(weight_t[...], both)
    wide = values.astype(f32)
    own[...] = jnp.concatenate(head_rows(wide, attention_column(att_dst_in[...])), axis=0)
    own_cross[...] = jnp.concatenate(head_rows(wide, column), axis=0)
    own_self[...] = values
    spread[...] = column
    score_ref[me] = own[...]
    cross_ref[0] = own_cross[...]
    self_ref[0] = own_self[pl.ds(pl.multiple_of(core * HALF, HALF), HALF), :]

    pl.semaphore_wait(barrier, n_col - 1)

    def score_copy(target, source_slot):
        return pltpu.make_async_remote_copy(
            src_ref=own, dst_ref=score_ref.at[me], send_sem=send_sem.at[target], recv_sem=recv_sem.at[source_slot],
            device_id={"col": target}, device_id_type=pl.DeviceIdType.MESH)

    def send(step, carry):
        score_copy(lax.rem(me + step, n_col), me).start()
        return carry

    lax.fori_loop(1, n_col, send, 0)
    self_copy = pltpu.make_async_remote_copy(
        src_ref=own_self.at[pl.ds(pl.multiple_of((1 - core) * HALF, HALF), HALF), :], dst_ref=self_ref.at[1],
        send_sem=part_send.at[0], recv_sem=part_recv.at[0],
        device_id={"col": partner}, device_id_type=pl.DeviceIdType.MESH)
    cross_copy = pltpu.make_async_remote_copy(
        src_ref=own_cross, dst_ref=cross_ref.at[1], send_sem=part_send.at[1], recv_sem=part_recv.at[1],
        device_id={"col": partner}, device_id_type=pl.DeviceIdType.MESH)
    self_copy.start()
    cross_copy.start()

    loads[-1].wait()
    n_cols = scaled.shape[0]
    wide_block = 2 * TILE

    def source_block(step, carry):
        low, high = carry
        at = pl.multiple_of(step * wide_block, wide_block)
        values = project_rows_t(weight_t[...], feat_in[pl.ds(at, wide_block), :]).astype(f32)
        pad = jnp.zeros((14, TILE), f32)
        for part in range(2):
            block = 2 * step + part
            here = values[:, part * TILE : (part + 1) * TILE]
            rows = head_rows(here, spread[...])
            for h in range(HEADS):
                grow = jnp.exp(rows[h])
                fall = jnp.exp(-0.8 * rows[h])
                grow_high = grow.astype(bf16).astype(f32)
                scaled[block, h, 0:HEAD_DIM, :] = (here[h * HEAD_DIM : (h + 1) * HEAD_DIM] * grow).astype(bf16)
                scaled[block, h, HEAD_DIM:AUG, :] = jnp.concatenate(
                    [grow_high, grow - grow_high, pad], axis=0).astype(bf16)
                ratio[block, h] = jnp.broadcast_to(fall, (16, TILE)).astype(bf16)
            stacked = jnp.concatenate(rows, axis=0)
            src_score[block] = stacked
            low, high = jnp.minimum(low, stacked), jnp.maximum(high, stacked)
        return low, high

    low, high = lax.fori_loop(0, n_cols // 2, source_block,
                              (jnp.full((HEADS, TILE), 1e30, f32), jnp.full((HEADS, TILE), -1e30, f32)))
    range_ref[0] = low
    range_ref[1] = high

    slots = rows_in.shape[1]
    row_block = rows_in[...].astype(f32)
    slot = lax.broadcasted_iota(jnp.int32, (1, slots), 1)
    row_block = jnp.where(slot < count_in[...], row_block, 255.0)
    pad = jnp.full((1, ORDER - slots), 255.0, f32)
    row_block = jnp.concatenate([row_block, pad], axis=1)
    across = jnp.broadcast_to(row_block, (ORDER, ORDER))
    down = jnp.transpose(across)
    lane = lax.broadcasted_iota(jnp.int32, (ORDER, ORDER), 1)
    sub = lax.broadcasted_iota(jnp.int32, (ORDER, ORDER), 0)
    before = jnp.sum(jnp.where((down == across) & (sub < lane), 1.0, 0.0), axis=0, keepdims=True)
    block_id = lax.broadcasted_iota(jnp.int32, (16, ORDER), 0).astype(f32)
    counts = jnp.sum(jnp.where(block_id == row_block, 1.0, 0.0), axis=1, keepdims=True)
    pairs = jnp.floor((counts + 1.0) * 0.5)
    start = jnp.sum(jnp.where(block_id < row_block, pairs, 0.0), axis=0, keepdims=True)
    place = jnp.where(row_block < 254.0, 2.0 * start + before, -1.0)
    place_down = jnp.transpose(jnp.broadcast_to(place, (ORDER, ORDER)))
    columns = jnp.concatenate([cols_in[...].astype(f32), jnp.zeros((1, ORDER - slots), f32)], axis=1)
    lane_row = lax.broadcasted_iota(jnp.int32, (1, ORDER), 1).astype(f32)
    code = 1.0 + lane_row + 256.0 * columns + 8192.0 * jnp.minimum(row_block, 15.0)
    code_down = jnp.transpose(jnp.broadcast_to(code, (ORDER, ORDER)))
    found = jnp.sum(jnp.where(place_down == lane.astype(f32), code_down, 0.0), axis=0, keepdims=True)
    order_ref[...] = found.astype(jnp.int32)
    pairs_ref[...] = jnp.broadcast_to(jnp.sum(pairs, axis=0, keepdims=True), (1, 128)).astype(jnp.int32)

    def finish(step, carry):
        peer = lax.rem(me + step, n_col)
        done = score_copy(peer, peer)
        done.wait_send()
        done.wait_recv()
        return carry

    lax.fori_loop(1, n_col, finish, 0)
    self_copy.wait()
    cross_copy.wait()


def edges_kernel(order_ref, pairs_ref, score_ref, scaled, ratio, src_score, range_ref, feat_hbm, weight_hbm, mask_hbm,
                 out_ref, ratio_dst, dst_score, acc, masks, feat_in, weight_in, mask_sem, load_sem):
    n_blocks = acc.shape[0]
    total = pairs_ref[0, 0]
    groups = (total + GROUP - 1) // GROUP

    def decode(position):
        code = order_ref[0, position]
        index = jnp.maximum(code - 1, 0)
        return code, index & 255, (index >> 8) & 31, index >> 13

    def mask_copy(pair, side, slot_at):
        ring = lax.rem(pair, RING)
        return pltpu.make_async_copy(mask_hbm.at[slot_at], masks.at[ring, side], mask_sem.at[ring, side])

    def fetch(pair):
        for side in range(2):
            code, slot, _, _ = decode(2 * pair + side)

            @pl.when(code > 0)
            def _(side=side, slot=slot):
                mask_copy(pair, side, slot).start()

            @pl.when(code == 0)
            def _(side=side):
                masks[lax.rem(pair, RING), side] = jnp.zeros((TILE, TILE), jnp.int32)

    def arrive(pair):
        for side in range(2):
            @pl.when(decode(2 * pair + side)[0] > 0)
            def _(side=side):
                mask_copy(pair, side, 0).wait()

    def prefetch(pair, carry):
        fetch(pair)
        return carry

    lax.fori_loop(0, jnp.minimum(groups * GROUP, RING - GROUP), prefetch, 0)

    spread_head = lax.broadcasted_iota(jnp.int32, (HEADS, HEADS * TILE), 0)
    spread_lane = lax.broadcasted_iota(jnp.int32, (HEADS, HEADS * TILE), 1) // TILE
    spread = jnp.where(spread_head == spread_lane, 1.0, 0.0).astype(bf16)

    def dst_block(step, carry):
        low, high = carry
        for part in range(4):
            block = 4 * step + part
            score = score_ref[2 * block] + score_ref[2 * block + 1]
            dst_score[block] = score
            fall = jnp.exp(-0.8 * score).astype(bf16)
            wide = transposed_dot(fall, spread).astype(bf16)
            for h in range(HEADS):
                ratio_dst[block, h] = wide[:, h * TILE : (h + 1) * TILE]
            acc[block] = jnp.zeros(acc.shape[1:], f32)
            low, high = jnp.minimum(low, score), jnp.maximum(high, score)
        return low, high

    low, high = lax.fori_loop(0, n_blocks // 4, dst_block, (range_ref[0], range_ref[1]))
    factored = (jnp.max(high) <= SPAN) & (jnp.min(low) >= -SPAN)

    def next_group(group):
        for step in range(GROUP):
            pair = group * GROUP + step

            @pl.when(pair + RING - GROUP < groups * GROUP)
            def _():
                fetch(pair + RING - GROUP)

            arrive(pair)

    @pl.when(factored)
    def _():
        def group_step(group, carry):
            next_group(group)
            one = jnp.ones((), bf16)
            for step in range(GROUP):
                pair = group * GROUP + step
                _, _, col_a, block = decode(2 * pair)
                _, _, col_b, _ = decode(2 * pair + 1)
                ring = lax.rem(pair, RING)
                mask_a = masks[ring, 0].astype(f32).astype(bf16).reshape(8, 16, TILE)
                mask_b = masks[ring, 1].astype(f32).astype(bf16).reshape(8, 16, TILE)
                for h in range(HEADS):
                    fall_dst = ratio_dst[block, h].reshape(8, 16, TILE)
                    weight_a = jnp.maximum(fall_dst * ratio[col_a, h][None], one) * mask_a
                    weight_b = jnp.maximum(fall_dst * ratio[col_b, h][None], one) * mask_b
                    edge = jnp.concatenate([weight_a.reshape(TILE, TILE), weight_b.reshape(TILE, TILE)], axis=1)
                    source = jnp.concatenate([scaled[col_a, h], scaled[col_b, h]], axis=1)
                    acc[block, h] += lax.dot_general(source, edge, (((1,), (1,)), ((), ())),
                                                     preferred_element_type=f32)
            return carry

        lax.fori_loop(0, groups, group_step, 0)

        def reference_rows(block, carry):
            for h in range(HEADS):
                acc[block, h, 66:67, :] = dst_score[block, h : h + 1, :]
            return carry

        lax.fori_loop(0, n_blocks, reference_rows, 0)

    @pl.when(jnp.logical_not(factored))
    def _():
        loads = [pltpu.make_async_copy(feat_hbm, feat_in, load_sem.at[0]),
                 pltpu.make_async_copy(weight_hbm, weight_in, load_sem.at[1])]
        for load in loads:
            load.start()
        for load in loads:
            load.wait()

        def empty_rows(block, carry):
            for h in range(HEADS):
                acc[block, h, 66:67, :] = jnp.full((1, TILE), NEG, f32)
            return carry

        lax.fori_loop(0, n_blocks, empty_rows, 0)

        def one_tile(ring, side, col, block):
            present = jnp.transpose(masks[ring, side].astype(f32)) > 0.0
            at = pl.multiple_of(col * TILE, TILE)
            values = project_t(weight_in[...], feat_in[pl.ds(at, TILE), :])
            for h in range(HEADS):
                source = as_column(src_score[col, h : h + 1, :], TILE)
                logit = leaky_relu(source + dst_score[block, h : h + 1, :])
                logit = jnp.where(present, logit, NEG)
                old_max = acc[block, h, 66:67, :]
                new_max = jnp.maximum(old_max, jnp.max(logit, axis=0, keepdims=True))
                prob = jnp.where(present, jnp.exp(logit - new_max), 0.0)
                keep = jnp.exp(old_max - new_max)
                message = jnp.dot(values[h * HEAD_DIM : (h + 1) * HEAD_DIM], prob.astype(bf16),
                                  preferred_element_type=f32)
                acc[block, h, 0:HEAD_DIM, :] = acc[block, h, 0:HEAD_DIM, :] * keep + message
                acc[block, h, 64:65, :] = acc[block, h, 64:65, :] * keep + jnp.sum(prob, axis=0, keepdims=True)
                acc[block, h, 66:67, :] = new_max

        def group_step(group, carry):
            next_group(group)

            def pair_step(step, inner):
                pair = group * GROUP + step
                ring = lax.rem(pair, RING)
                for side in range(2):
                    _, _, col, _ = decode(2 * pair + side)
                    one_tile(ring, side, col, decode(2 * pair)[3])
                return inner

            return lax.fori_loop(0, GROUP, pair_step, carry)

        lax.fori_loop(0, groups, group_step, 0)

    def store_block(step, carry):
        for part in range(2):
            block = 2 * step + part
            for half in range(2):
                logs = []
                for g in range(HALF_HEADS):
                    h = half * HALF_HEADS + g
                    denominator = acc[block, h, 64:65, :] + acc[block, h, 65:66, :]
                    some = denominator > 0.0
                    safe = jnp.where(some, denominator, 1.0)
                    out_ref[half, block, g * HEAD_DIM : (g + 1) * HEAD_DIM, :] = (
                        acc[block, h, 0:HEAD_DIM, :] * (1.0 / safe)).astype(bf16)
                    logs.append(jnp.where(some, acc[block, h, 66:67, :] + jnp.log(safe), NEG))
                out_ref[half, block, HALF:BLOCK, :] = pack_logs(jnp.concatenate(logs, axis=0))
        return carry

    lax.fori_loop(0, n_blocks // 2, store_block, 0)


def pack_logs(logs):
    high, middle, low = [part.astype(f32) for part in split3(logs)]
    return jnp.concatenate([high, middle, low, jnp.zeros_like(high)], axis=0).astype(bf16)


def unpack_logs(rows):
    wide = rows.astype(f32)
    n = HALF_HEADS
    return wide[0:n] + wide[n : 2 * n] + wide[2 * n : 3 * n]


def merge_blocks(blocks):
    logs = [unpack_logs(block[HALF:BLOCK]) for block in blocks]
    top = functools.reduce(jnp.maximum, logs)
    grow = [jnp.exp(log - top) for log in logs]
    total = functools.reduce(jnp.add, grow)
    share = [g * (1.0 / total) for g in grow]
    parts = []
    for h in range(HALF_HEADS):
        at = slice(h * HEAD_DIM, (h + 1) * HEAD_DIM)
        terms = [block[at].astype(f32) * s[h : h + 1] for block, s in zip(blocks, share)]
        parts.append(functools.reduce(jnp.add, terms).astype(bf16))
    return parts, pack_logs(top + jnp.log(total))


def store_block_parts(ref, index, merged):
    parts, logs = merged
    for h, part in enumerate(parts):
        ref[index + (slice(h * HEAD_DIM, (h + 1) * HEAD_DIM), slice(None))] = part
    ref[index + (slice(HALF, BLOCK), slice(None))] = logs


def merge_kernel(n_y, n_z, part_ref, score_ref, self_ref, cross_ref, bias_hbm, out_ref,
                 pair_in, summed, y_in, z_sum, z_in, self_logit, bias_in, fin, fin_in,
                 load_sem, pair_send, pair_recv, y_send, y_recv, z_send, z_recv, fin_send, fin_recv):
    me = lax.axis_index("col")
    core = lax.rem(me, 2)
    chip = me // 2
    y = lax.rem(chip, n_y)
    z = chip // n_y
    partner = me + 1 - 2 * core

    def at(z_at, y_at):
        return {"col": (z_at * n_y + y_at) * 2 + core}

    mesh_id = pl.DeviceIdType.MESH
    barrier = pltpu.get_barrier_semaphore()
    pl.semaphore_signal(barrier, inc=1, device_id={"col": partner}, device_id_type=mesh_id)
    for step in range(1, n_y):
        pl.semaphore_signal(barrier, inc=1, device_id=at(z, lax.rem(y + step, n_y)), device_id_type=mesh_id)
    for step in range(1, n_z):
        pl.semaphore_signal(barrier, inc=1, device_id=at(lax.rem(z + step, n_z), y), device_id_type=mesh_id)

    def z_of(step):
        return lax.rem(z + 1 + step, n_z)

    def pair_copy(step):
        rows = pl.ds(z_of(step) * n_y, n_y)
        return pltpu.make_async_remote_copy(
            src_ref=part_ref.at[1 - core, rows], dst_ref=pair_in.at[rows], send_sem=pair_send.at[step],
            recv_sem=pair_recv.at[step], device_id={"col": partner}, device_id_type=mesh_id)

    def y_copy(step, dy):
        block = z_of(step) * n_y + lax.rem(y + dy, n_y)
        return pltpu.make_async_remote_copy(
            src_ref=summed.at[block], dst_ref=y_in.at[step, dy - 1], send_sem=y_send.at[step, dy - 1],
            recv_sem=y_recv.at[step, dy - 1], device_id=at(z, lax.rem(y + dy, n_y)), device_id_type=mesh_id)

    def z_copy(step):
        return pltpu.make_async_remote_copy(
            src_ref=z_sum.at[step], dst_ref=z_in.at[step], send_sem=z_send.at[step],
            recv_sem=z_recv.at[step], device_id=at(z_of(step), y), device_id_type=mesh_id)

    bias_copy = pltpu.make_async_copy(bias_hbm, bias_in, load_sem)
    bias_copy.start()
    direct = score_ref[2 * chip] + score_ref[2 * chip + 1]
    logit = leaky_relu(direct + (cross_ref[0] + cross_ref[1]))
    self_logit[0] = logit
    self_logit[1] = jnp.concatenate([logit[HALF_HEADS:], logit[:HALF_HEADS]], axis=0)

    pl.semaphore_wait(barrier, 1 + (n_y - 1) + (n_z - 1))
    for step in range(n_z):
        pair_copy(step).start()

    def pair_merge(step):
        pair_copy(step).wait()
        for dy in range(n_y):
            block = z_of(step) * n_y + lax.rem(y + dy, n_y)
            store_block_parts(summed, (block,), merge_blocks([part_ref[core, block], pair_in[block]]))
        for dy in range(1, n_y):
            y_copy(step, dy).start()

    def y_merge(step):
        for dy in range(1, n_y):
            y_copy(step, dy).wait()
        blocks = [summed[z_of(step) * n_y + y]] + [y_in[step, dy - 1] for dy in range(1, n_y)]
        store_block_parts(z_sum, (step,), merge_blocks(blocks))
        if step < n_z - 1:
            z_copy(step).start()

    for step in range(n_z):
        pair_merge(step)
        if step > 0:
            y_merge(step - 1)
    y_merge(n_z - 1)
    for step in range(n_z - 1):
        z_copy(step).wait()

    blocks = [z_sum[n_z - 1]] + [z_in[step] for step in range(n_z - 1)]
    logs = [unpack_logs(block[HALF:BLOCK]) for block in blocks] + [self_logit[core][0:HALF_HEADS]]
    top = functools.reduce(jnp.maximum, logs)
    grow = [jnp.exp(log - top) for log in logs]
    inverse = 1.0 / functools.reduce(jnp.add, grow)
    pieces = []
    for h in range(HALF_HEADS):
        rows = slice(h * HEAD_DIM, (h + 1) * HEAD_DIM)
        terms = [block[rows].astype(f32) * g[h : h + 1] for block, g in zip(blocks, grow)]
        mine = self_ref[0, rows, :].astype(f32) + self_ref[1, rows, :].astype(f32)
        terms.append(mine * grow[-1][h : h + 1])
        pieces.append(functools.reduce(jnp.add, terms) * inverse[h : h + 1])
    mixed = jnp.transpose(jnp.concatenate(pieces, axis=0))
    bias_copy.wait()
    bias = jnp.where(core == 0, bias_in[:, 0:HALF], bias_in[:, HALF:FEAT])
    mixed = mixed + bias
    fin[...] = jnp.where(mixed > 0, mixed, jnp.exp(jnp.minimum(mixed, 0.0)) - 1.0)
    half = out_ref.shape[0]
    final = pltpu.make_async_remote_copy(
        src_ref=fin.at[pl.ds(pl.multiple_of((1 - core) * half, half), half), :], dst_ref=fin_in,
        send_sem=fin_send, recv_sem=fin_recv, device_id={"col": partner}, device_id_type=mesh_id)
    final.start()
    mine = fin[pl.ds(pl.multiple_of(core * half, half), half), :]
    final.wait()
    theirs = fin_in[...]
    out_ref[:, 0:HALF] = jnp.where(core == 0, mine, theirs)
    out_ref[:, HALF:FEAT] = jnp.where(core == 0, theirs, mine)


VMEM = pl.BlockSpec(memory_space=pltpu.VMEM)
SMEM = pl.BlockSpec(memory_space=pltpu.SMEM)
HBM = pl.BlockSpec(memory_space=pltpu.HBM)
DMA = pltpu.SemaphoreType.DMA


MIB = 1024 * 1024


def scores_and_tables(n_col, dst_feat, weight, att_src, att_dst, tile_rows, tile_cols, tile_count, src_feat):
    own = dst_feat.shape[0]
    chip = 2 * own
    n_cols = src_feat.shape[0] // TILE
    return pl.pallas_call(
        functools.partial(scores_kernel, n_col),
        name="scores_and_tables",
        out_shape=(
            jax.ShapeDtypeStruct((n_col, HEADS, chip), f32),
            jax.ShapeDtypeStruct((2, HALF, chip), bf16),
            jax.ShapeDtypeStruct((2, HEADS, chip), f32),
            jax.ShapeDtypeStruct((1, ORDER), jnp.int32),
            jax.ShapeDtypeStruct((1, 128), jnp.int32),
            jax.ShapeDtypeStruct((n_cols, HEADS, AUG, TILE), bf16),
            jax.ShapeDtypeStruct((n_cols, HEADS, 16, TILE), bf16),
            jax.ShapeDtypeStruct((n_cols, HEADS, TILE), f32),
            jax.ShapeDtypeStruct((2, HEADS, TILE), f32),
        ),
        in_specs=[HBM] * 8,
        out_specs=(VMEM,) * 9,
        scratch_shapes=[
            pltpu.VMEM(dst_feat.shape, bf16), pltpu.VMEM(weight.shape, bf16),
            pltpu.VMEM(att_src.shape, f32), pltpu.VMEM(att_dst.shape, f32),
            pltpu.VMEM(tile_rows.shape, jnp.int32), pltpu.VMEM(tile_cols.shape, jnp.int32),
            pltpu.VMEM(tile_count.shape, jnp.int32), pltpu.VMEM(src_feat.shape, bf16),
            pltpu.VMEM((HEADS, chip), f32), pltpu.VMEM((HEADS, chip), f32), pltpu.VMEM((FEAT, chip), bf16),
            pltpu.VMEM((FEAT, weight.shape[0]), bf16), pltpu.VMEM((FEAT, TILE), f32),
            DMA((8,)), DMA((n_col,)), DMA((n_col,)), DMA((2,)), DMA((2,)),
        ],
        compiler_params=pltpu.CompilerParams(collective_id=0, has_side_effects=True, vmem_limit_bytes=40 * MIB),
    )(dst_feat, weight, att_src, att_dst, tile_rows, tile_cols, tile_count, src_feat)


def edge_sums(order, pairs, scores, scaled, ratio, src_score, span, src_feat, weight, masks):
    n_blocks = scores.shape[0] // 2
    return pl.pallas_call(
        edges_kernel,
        name="edge_sums",
        out_shape=jax.ShapeDtypeStruct((2, n_blocks, BLOCK, TILE), bf16),
        in_specs=[SMEM, SMEM] + [VMEM] * 5 + [HBM] * 3,
        out_specs=VMEM,
        scratch_shapes=[
            pltpu.VMEM((n_blocks, HEADS, TILE, TILE), bf16),
            pltpu.VMEM((n_blocks, HEADS, TILE), f32),
            pltpu.VMEM((n_blocks, HEADS, AUG, TILE), f32),
            pltpu.VMEM((RING, 2, TILE, TILE), jnp.int32),
            pltpu.VMEM(src_feat.shape, bf16),
            pltpu.VMEM(weight.shape, bf16),
            DMA((RING, 2)), DMA((2,)),
        ],
        compiler_params=pltpu.CompilerParams(vmem_limit_bytes=40 * MIB),
    )(order, pairs, scores, scaled, ratio, src_score, span, src_feat, weight, masks)


def merge(n_y, n_z, parts, scores, self_values, cross, bias):
    n_blocks = n_y * n_z
    own = scores.shape[2] // 2
    return pl.pallas_call(
        functools.partial(merge_kernel, n_y, n_z),
        name="merge",
        out_shape=jax.ShapeDtypeStruct((own, FEAT), f32),
        in_specs=[VMEM] * 4 + [HBM],
        out_specs=VMEM,
        scratch_shapes=[
            pltpu.VMEM((n_blocks, BLOCK, TILE), bf16),
            pltpu.VMEM((n_blocks, BLOCK, TILE), bf16),
            pltpu.VMEM((n_z, n_y - 1, BLOCK, TILE), bf16),
            pltpu.VMEM((n_z, BLOCK, TILE), bf16),
            pltpu.VMEM((n_z - 1, BLOCK, TILE), bf16),
            pltpu.VMEM((2, HEADS, TILE), f32),
            pltpu.VMEM((1, FEAT), f32),
            pltpu.VMEM((TILE, HALF), f32),
            pltpu.VMEM((own, HALF), f32),
            DMA(()), DMA((n_z,)), DMA((n_z,)), DMA((n_z, n_y - 1)), DMA((n_z, n_y - 1)),
            DMA((n_z - 1,)), DMA((n_z - 1,)), DMA(()), DMA(()),
        ],
        compiler_params=pltpu.CompilerParams(collective_id=1, has_side_effects=True, vmem_limit_bytes=40 * MIB),
    )(parts, scores, self_values, cross, bias)


def local(n_col, src_feat, dst_feat, weight, att_src, att_dst, bias, tile_rows, tile_cols, tile_masks, tile_count):
    slots = tile_rows.shape[2]
    tile_rows, tile_cols, bias = tile_rows.reshape(1, slots), tile_cols.reshape(1, slots), bias.reshape(1, FEAT)
    tile_masks = tile_masks.reshape(slots, TILE, TILE)
    (src_feat, dst_feat, weight, att_src, att_dst, bias, tile_rows, tile_cols, tile_masks) = [
        pltpu.with_memory_space_constraint(array, pltpu.HBM)
        for array in (src_feat, dst_feat, weight, att_src, att_dst, bias, tile_rows, tile_cols, tile_masks)
    ]
    scores, self_values, cross, order, pairs, scaled, ratio, src_score, span = scores_and_tables(
        n_col, dst_feat, weight, att_src, att_dst, tile_rows, tile_cols, tile_count, src_feat)
    parts = edge_sums(order, pairs, scores, scaled, ratio, src_score, span, src_feat, weight, tile_masks)
    n_y = 4
    return merge(n_y, n_col // (2 * n_y), parts, scores, self_values, cross, bias)


def solution(mesh):
    placed = (
        P("col", None),
        P(("row", "col"), None),
        P(),
        P(),
        P(),
        P(),
        P("row", "col", None),
        P("row", "col", None),
        P("row", "col", None, None, None),
        P("row", "col"),
    )
    return jax.shard_map(
        functools.partial(local, mesh.shape["col"]), mesh=mesh, in_specs=placed,
        out_specs=P(("row", "col"), None), check_vma=False,
    )
```

time: 125 us -> 111 us (0.89)
  Pallas kernels: 116 us -> 109 us
  local copies, waits for them, and re-layouts: 7.13 us -> 0.66 us
    pallas_call x1, Pallas kernels: 64.2 us -> 45 us  [edge_sums(): pl.pallas_call(edges_kernel, name='edge_sums', out_shape=jax.ShapeDtypeSt...]
    pallas_call x1, Pallas kernels: 40.2 us -> 49.5 us  [merge(): pl.pallas_call(functools.partial(merge_kernel, n_y, n_z), name='merge', o...]
    unnamed x21 -> x1, local copies, waits for them, and re-layouts: 7.13 us -> 0.66 us
    pallas_call x1, Pallas kernels: 12.1 us -> 14.2 us  [scores_and_tables(): pl.pallas_call(functools.partial(scores_kernel, n_col), name='scores_and_...]
where the time goes in v2:
time: 111 us; the launch traced here: 110 us
  Pallas kernels  109 us (98%)
    pallas_call x1, Pallas kernels, merge(): pl.pallas_call(functools.partial(merge_kernel, n_y, n_z), name='merge', o...  49.5 us
    pallas_call x1, Pallas kernels, edge_sums(): pl.pallas_call(edges_kernel, name='edge_sums', out_shape=jax.ShapeDtypeSt...  45 us
    pallas_call x1, Pallas kernels, scores_and_tables(): pl.pallas_call(functools.partial(scores_kernel, n_col), name='scores_and_...  14.2 us

profile of v2, /device:TPU:7, one launch (start us, length us, event | category | flops | bytes accessed | tf_op | source)
XLA Modules:
  0.0 110.1 jit_solution(15797590378818256172)
XLA Ops:
  0.7 14.2 %scores_and_tables.1 = (f32[32,8,128]{2,1,0:T(8,128)S(1)}, bf16[2,256,128]{2,1,0:T(8,128)(2,1)S(1)}, f32[2,8,128]{2,1,0:T(8,128)S(1)}, s32[1,256]{1,0:T(1,128)S(...) custom-call(bf16[64,128]{1,0:T(8,128)(2,1)} %dst_hbm.1, ...), custom_call_target="tpu_custom_call" | custom-call | tf_op jit(solution)/shard_map/scores_and_tables/pallas_call | solution.py:524
  14.9 45.0 %edge_sums.1.part_ref = bf16[2,16,272,128]{3,2,1,0:T(8,128)(2,1)S(1)} custom-call(s32[1,256]{1,0:T(1,128)S(1)} %get-tuple-element.14.order_ref, s32[1,128]{1,0:T(1,128)S(1)} %get-tuple-element.15.pairs_ref, f32[32,8,128]{2,1,0:T(8,128)S(1)} %get-tuple-element.16.score_ref, bf16[32,8,80,128]{3,2,1,0:T(8,128)(2,1)S(1)} %get-tuple-element.17.scaled, ...), custom_call_target="tpu_custom_call" | custom-call | tf_op jit(solution)/shard_map/edge_sums/pallas_call | solution.py:555
  60.0 49.5 %merge.1 = f32[64,512]{1,0:T(8,128)S(1)} custom-call(bf16[2,16,272,128]{3,2,1,0:T(8,128)(2,1)S(1)} %edge_sums.1.part_ref, f32[32,8,128]{2,1,0:T(8,128)S(1)} %get-tuple-element.16.score_ref, bf16[2,256,128]{2,1,0:T(8,128)(2,1)S(1)} %get-tuple-element.21.self_ref, f32[2,8,128]{2,1,0:T(8,128)S(1)} %get-tuple-element.22.cross_ref, f32[1,512]{1,0:T(1,128)} %bitcast.5), custom_call_target="tpu_custom_call" | custom-call | tf_op jit(solution)/shard_map/merge/pallas_call | solution.py:577
  109.4 0.7 copy.13

commit v3 on v2

--- a/solution.py
+++ b/solution.py
@@ -17,8 +17,8 @@
 HALF_HEADS = HEADS // 2
 BLOCK = HALF + 16
 AUG = HEAD_DIM + 16
-GROUP = 4
-RING = 16
+GROUP = 8
+RING = 32
 ORDER = 256
 
 f32 = jnp.float32
@@ -213,27 +213,18 @@
         index = jnp.maximum(code - 1, 0)
         return code, index & 255, (index >> 8) & 31, index >> 13
 
-    def mask_copy(pair, side, slot_at):
+    def fetch(pair):
         ring = lax.rem(pair, RING)
-        return pltpu.make_async_copy(mask_hbm.at[slot_at], masks.at[ring, side], mask_sem.at[ring, side])
-
-    def fetch(pair):
         for side in range(2):
-            code, slot, _, _ = decode(2 * pair + side)
-
-            @pl.when(code > 0)
-            def _(side=side, slot=slot):
-                mask_copy(pair, side, slot).start()
-
-            @pl.when(code == 0)
-            def _(side=side):
-                masks[lax.rem(pair, RING), side] = jnp.zeros((TILE, TILE), jnp.int32)
+            slot = decode(2 * pair + side)[1]
+            pltpu.make_async_copy(mask_hbm.at[slot], masks.at[ring, side], mask_sem.at[ring]).start()
 
     def arrive(pair):
-        for side in range(2):
-            @pl.when(decode(2 * pair + side)[0] > 0)
-            def _(side=side):
-                mask_copy(pair, side, 0).wait()
+        ring = lax.rem(pair, RING)
+        pltpu.make_async_copy(mask_hbm.at[pl.ds(0, 2)], masks.at[ring], mask_sem.at[ring]).wait()
+
+    def mask_of(ring, side, code):
+        return masks[ring, side].astype(f32) * jnp.minimum(code, 1).astype(f32)
 
     def prefetch(pair, carry):
         fetch(pair)
@@ -263,14 +254,13 @@
     factored = (jnp.max(high) <= SPAN) & (jnp.min(low) >= -SPAN)
 
     def next_group(group):
+        @pl.when((group + 1) * GROUP + RING - 2 * GROUP < groups * GROUP)
+        def _():
+            for step in range(GROUP):
+                fetch(group * GROUP + step + RING - GROUP)
+
         for step in range(GROUP):
-            pair = group * GROUP + step
-
-            @pl.when(pair + RING - GROUP < groups * GROUP)
-            def _():
-                fetch(pair + RING - GROUP)
-
-            arrive(pair)
+            arrive(group * GROUP + step)
 
     @pl.when(factored)
     def _():
@@ -279,11 +269,11 @@
             one = jnp.ones((), bf16)
             for step in range(GROUP):
                 pair = group * GROUP + step
-                _, _, col_a, block = decode(2 * pair)
-                _, _, col_b, _ = decode(2 * pair + 1)
+                code_a, _, col_a, block = decode(2 * pair)
+                code_b, _, col_b, _ = decode(2 * pair + 1)
                 ring = lax.rem(pair, RING)
-                mask_a = masks[ring, 0].astype(f32).astype(bf16).reshape(8, 16, TILE)
-                mask_b = masks[ring, 1].astype(f32).astype(bf16).reshape(8, 16, TILE)
+                mask_a = mask_of(ring, 0, code_a).astype(bf16).reshape(8, 16, TILE)
+                mask_b = mask_of(ring, 1, code_b).astype(bf16).reshape(8, 16, TILE)
                 for h in range(HEADS):
                     fall_dst = ratio_dst[block, h].reshape(8, 16, TILE)
                     weight_a = jnp.maximum(fall_dst * ratio[col_a, h][None], one) * mask_a
@@ -319,8 +309,8 @@
 
         lax.fori_loop(0, n_blocks, empty_rows, 0)
 
-        def one_tile(ring, side, col, block):
-            present = jnp.transpose(masks[ring, side].astype(f32)) > 0.0
+        def one_tile(ring, side, code, col, block):
+            present = jnp.transpose(mask_of(ring, side, code)) > 0.0
             at = pl.multiple_of(col * TILE, TILE)
             values = project_t(weight_in[...], feat_in[pl.ds(at, TILE), :])
             for h in range(HEADS):
@@ -344,8 +334,8 @@
                 pair = group * GROUP + step
                 ring = lax.rem(pair, RING)
                 for side in range(2):
-                    _, _, col, _ = decode(2 * pair + side)
-                    one_tile(ring, side, col, decode(2 * pair)[3])
+                    code, _, col, _ = decode(2 * pair + side)
+                    one_tile(ring, side, code, col, decode(2 * pair)[3])
                 return inner
 
             return lax.fori_loop(0, GROUP, pair_step, carry)
@@ -565,7 +555,7 @@
             pltpu.VMEM((RING, 2, TILE, TILE), jnp.int32),
             pltpu.VMEM(src_feat.shape, bf16),
             pltpu.VMEM(weight.shape, bf16),
-            DMA((RING, 2)), DMA((2,)),
+            DMA((RING,)), DMA((2,)),
         ],
         compiler_params=pltpu.CompilerParams(vmem_limit_bytes=40 * MIB),
     )(order, pairs, scores, scaled, ratio, src_score, span, src_feat, weight, masks)

time: 111 us -> 115 us (1.036)
  Pallas kernels: 109 us -> 112 us
    pallas_call x1, Pallas kernels: 49.5 us -> 60.4 us  [merge(): pl.pallas_call(functools.partial(merge_kernel, n_y, n_z), name='merge', o...]
    pallas_call x1, Pallas kernels: 45 us -> 37.7 us  [edge_sums(): pl.pallas_call(edges_kernel, name='edge_sums', out_shape=jax.ShapeDtypeSt...]
where the time goes in v3:
time: 115 us; the launch traced here: 114 us
  Pallas kernels  112 us (97%)
    pallas_call x1, Pallas kernels, merge(): pl.pallas_call(functools.partial(merge_kernel, n_y, n_z), name='merge', o...  60.4 us
    pallas_call x1, Pallas kernels, edge_sums(): pl.pallas_call(edges_kernel, name='edge_sums', out_shape=jax.ShapeDtypeSt...  37.7 us
    pallas_call x1, Pallas kernels, scores_and_tables(): pl.pallas_call(functools.partial(scores_kernel, n_col), name='scores_and_...  14.2 us

profile of v3, /device:TPU:7, one launch (start us, length us, event | category | flops | bytes accessed | tf_op | source)
XLA Modules:
  0.0 113.7 jit_solution(16918219983706115369)
XLA Ops:
  0.7 14.2 %scores_and_tables.1 = (f32[32,8,128]{2,1,0:T(8,128)S(1)}, bf16[2,256,128]{2,1,0:T(8,128)(2,1)S(1)}, f32[2,8,128]{2,1,0:T(8,128)S(1)}, s32[1,256]{1,0:T(1,128)S(...) custom-call(bf16[64,128]{1,0:T(8,128)(2,1)} %dst_hbm.1, ...), custom_call_target="tpu_custom_call" | custom-call | tf_op jit(solution)/shard_map/scores_and_tables/pallas_call | solution.py:514
  14.9 37.7 %edge_sums.1.part_ref = bf16[2,16,272,128]{3,2,1,0:T(8,128)(2,1)S(1)} custom-call(s32[1,256]{1,0:T(1,128)S(1)} %get-tuple-element.14.order_ref, s32[1,128]{1,0:T(1,128)S(1)} %get-tuple-element.15.pairs_ref, f32[32,8,128]{2,1,0:T(8,128)S(1)} %get-tuple-element.16.score_ref, bf16[32,8,80,128]{3,2,1,0:T(8,128)(2,1)S(1)} %get-tuple-element.17.scaled, ...), custom_call_target="tpu_custom_call" | custom-call | tf_op jit(solution)/shard_map/edge_sums/pallas_call | solution.py:545
  52.6 60.4 %merge.1 = f32[64,512]{1,0:T(8,128)S(1)} custom-call(bf16[2,16,272,128]{3,2,1,0:T(8,128)(2,1)S(1)} %edge_sums.1.part_ref, f32[32,8,128]{2,1,0:T(8,128)S(1)} %get-tuple-element.16.score_ref, bf16[2,256,128]{2,1,0:T(8,128)(2,1)S(1)} %get-tuple-element.21.self_ref, f32[2,8,128]{2,1,0:T(8,128)S(1)} %get-tuple-element.22.cross_ref, f32[1,512]{1,0:T(1,128)} %bitcast.5), custom_call_target="tpu_custom_call" | custom-call | tf_op jit(solution)/shard_map/merge/pallas_call | solution.py:567
  113.0 0.7 copy.13

commit v4 on v3

--- a/solution.py
+++ b/solution.py
@@ -69,14 +69,16 @@
     return jnp.transpose(jnp.broadcast_to(row, (rows, row.shape[1])))
 
 
-def scores_kernel(n_col, dst_hbm, weight_hbm, att_src_hbm, att_dst_hbm, rows_hbm, cols_hbm, count_hbm, feat_hbm,
+def scores_kernel(n_y, n_z, dst_hbm, weight_hbm, att_src_hbm, att_dst_hbm, rows_hbm, cols_hbm, count_hbm, feat_hbm,
                   score_ref, self_ref, cross_ref, order_ref, pairs_ref, scaled, ratio, src_score, range_ref,
                   dst_in, weight_in, att_src_in, att_dst_in, rows_in, cols_in, count_in, feat_in,
-                  own, own_cross, own_self, weight_t, spread,
-                  load_sem, send_sem, recv_sem, part_send, part_recv):
+                  own, own_cross, own_self, weight_t, spread, pair_in,
+                  load_sem, y_send, y_recv, z_send, z_recv, part_send, part_recv):
     me = lax.axis_index("col")
     core = lax.rem(me, 2)
     partner = me + 1 - 2 * core
+    chip = me // 2
+    y, z = lax.rem(chip, n_y), chip // n_y
     loads = [
         pltpu.make_async_copy(source, target, load_sem.at[i])
         for i, (source, target) in enumerate([
@@ -87,12 +89,15 @@
         load.start()
     barrier = pltpu.get_barrier_semaphore()
 
-    def greet(step, carry):
-        pl.semaphore_signal(barrier, inc=1, device_id={"col": lax.rem(me + step, n_col)},
-                            device_id_type=pl.DeviceIdType.MESH)
-        return carry
-
-    lax.fori_loop(1, n_col, greet, 0)
+    mesh_id = pl.DeviceIdType.MESH
+
+    def at(z_at, y_at):
+        return {"col": (z_at * n_y + y_at) * 2 + core}
+
+    y_peers = [at(z, lax.rem(y + step, n_y)) for step in range(1, n_y)]
+    z_peers = [at(lax.rem(z + step, n_z), y) for step in range(1, n_z)]
+    for peer in [{"col": partner}] + y_peers + z_peers:
+        pl.semaphore_signal(barrier, inc=1, device_id=peer, device_id_type=mesh_id)
     for load in loads[:-1]:
         load.wait()
 
@@ -108,43 +113,35 @@
     own_cross[...] = jnp.concatenate(head_rows(wide, column), axis=0)
     own_self[...] = values
     spread[...] = column
-    score_ref[me] = own[...]
     cross_ref[0] = own_cross[...]
     self_ref[0] = own_self[pl.ds(pl.multiple_of(core * HALF, HALF), HALF), :]
 
-    pl.semaphore_wait(barrier, n_col - 1)
-
-    def score_copy(target, source_slot):
-        return pltpu.make_async_remote_copy(
-            src_ref=own, dst_ref=score_ref.at[me], send_sem=send_sem.at[target], recv_sem=recv_sem.at[source_slot],
-            device_id={"col": target}, device_id_type=pl.DeviceIdType.MESH)
-
-    def send(step, carry):
-        score_copy(lax.rem(me + step, n_col), me).start()
-        return carry
-
-    lax.fori_loop(1, n_col, send, 0)
+    pl.semaphore_wait(barrier, 1 + len(y_peers) + len(z_peers))
+    pair_copy = pltpu.make_async_remote_copy(
+        src_ref=own, dst_ref=pair_in, send_sem=part_send.at[2], recv_sem=part_recv.at[2],
+        device_id={"col": partner}, device_id_type=mesh_id)
+    pair_copy.start()
     self_copy = pltpu.make_async_remote_copy(
         src_ref=own_self.at[pl.ds(pl.multiple_of((1 - core) * HALF, HALF), HALF), :], dst_ref=self_ref.at[1],
         send_sem=part_send.at[0], recv_sem=part_recv.at[0],
-        device_id={"col": partner}, device_id_type=pl.DeviceIdType.MESH)
+        device_id={"col": partner}, device_id_type=mesh_id)
     cross_copy = pltpu.make_async_remote_copy(
         src_ref=own_cross, dst_ref=cross_ref.at[1], send_sem=part_send.at[1], recv_sem=part_recv.at[1],
-        device_id={"col": partner}, device_id_type=pl.DeviceIdType.MESH)
+        device_id={"col": partner}, device_id_type=mesh_id)
     self_copy.start()
     cross_copy.start()
 
     loads[-1].wait()
     n_cols = scaled.shape[0]
-    wide_block = 2 * TILE
+    wide_block = 4 * TILE
 
     def source_block(step, carry):
         low, high = carry
         at = pl.multiple_of(step * wide_block, wide_block)
         values = project_rows_t(weight_t[...], feat_in[pl.ds(at, wide_block), :]).astype(f32)
         pad = jnp.zeros((14, TILE), f32)
-        for part in range(2):
-            block = 2 * step + part
+        for part in range(4):
+            block = 4 * step + part
             here = values[:, part * TILE : (part + 1) * TILE]
             rows = head_rows(here, spread[...])
             for h in range(HEADS):
@@ -160,8 +157,29 @@
             low, high = jnp.minimum(low, stacked), jnp.maximum(high, stacked)
         return low, high
 
-    low, high = lax.fori_loop(0, n_cols // 2, source_block,
-                              (jnp.full((HEADS, TILE), 1e30, f32), jnp.full((HEADS, TILE), -1e30, f32)))
+    def exchange(peers, rows, send_sem, recv_sem):
+        copies = [
+            pltpu.make_async_remote_copy(
+                src_ref=score_ref.at[rows], dst_ref=score_ref.at[rows], send_sem=send_sem.at[i],
+                recv_sem=recv_sem.at[i], device_id=peer, device_id_type=mesh_id)
+            for i, peer in enumerate(peers)
+        ]
+        for copy in copies:
+            copy.start()
+        return copies
+
+    steps = n_cols // 4
+    cuts = (0, steps // 4, (5 * steps) // 8, steps)
+    span = (jnp.full((HEADS, TILE), 1e30, f32), jnp.full((HEADS, TILE), -1e30, f32))
+    span = lax.fori_loop(cuts[0], cuts[1], source_block, span)
+    pair_copy.wait()
+    score_ref[chip] = own[...] + pair_in[...]
+    y_copies = exchange(y_peers, pl.ds(chip, 1), y_send, y_recv)
+    span = lax.fori_loop(cuts[1], cuts[2], source_block, span)
+    for copy in y_copies:
+        copy.wait()
+    z_copies = exchange(z_peers, pl.ds(z * n_y, n_y), z_send, z_recv)
+    low, high = lax.fori_loop(cuts[2], cuts[3], source_block, span)
     range_ref[0] = low
     range_ref[1] = high
 
@@ -190,14 +208,8 @@
     order_ref[...] = found.astype(jnp.int32)
     pairs_ref[...] = jnp.broadcast_to(jnp.sum(pairs, axis=0, keepdims=True), (1, 128)).astype(jnp.int32)
 
-    def finish(step, carry):
-        peer = lax.rem(me + step, n_col)
-        done = score_copy(peer, peer)
-        done.wait_send()
-        done.wait_recv()
-        return carry
-
-    lax.fori_loop(1, n_col, finish, 0)
+    for copy in z_copies:
+        copy.wait()
     self_copy.wait()
     cross_copy.wait()
 
@@ -240,7 +252,7 @@
         low, high = carry
         for part in range(4):
             block = 4 * step + part
-            score = score_ref[2 * block] + score_ref[2 * block + 1]
+            score = score_ref[block]
             dst_score[block] = score
             fall = jnp.exp(-0.8 * score).astype(bf16)
             wide = transposed_dot(fall, spread).astype(bf16)
@@ -343,8 +355,8 @@
         lax.fori_loop(0, groups, group_step, 0)
 
     def store_block(step, carry):
-        for part in range(2):
-            block = 2 * step + part
+        for part in range(4):
+            block = 4 * step + part
             for half in range(2):
                 logs = []
                 for g in range(HALF_HEADS):
@@ -358,7 +370,7 @@
                 out_ref[half, block, HALF:BLOCK, :] = pack_logs(jnp.concatenate(logs, axis=0))
         return carry
 
-    lax.fori_loop(0, n_blocks // 2, store_block, 0)
+    lax.fori_loop(0, n_blocks // 4, store_block, 0)
 
 
 def pack_logs(logs):
@@ -436,7 +448,7 @@
 
     bias_copy = pltpu.make_async_copy(bias_hbm, bias_in, load_sem)
     bias_copy.start()
-    direct = score_ref[2 * chip] + score_ref[2 * chip + 1]
+    direct = score_ref[chip]
     logit = leaky_relu(direct + (cross_ref[0] + cross_ref[1]))
     self_logit[0] = logit
     self_logit[1] = jnp.concatenate([logit[HALF_HEADS:], logit[:HALF_HEADS]], axis=0)
@@ -507,15 +519,15 @@
 MIB = 1024 * 1024
 
 
-def scores_and_tables(n_col, dst_feat, weight, att_src, att_dst, tile_rows, tile_cols, tile_count, src_feat):
+def scores_and_tables(n_y, n_z, dst_feat, weight, att_src, att_dst, tile_rows, tile_cols, tile_count, src_feat):
     own = dst_feat.shape[0]
     chip = 2 * own
     n_cols = src_feat.shape[0] // TILE
     return pl.pallas_call(
-        functools.partial(scores_kernel, n_col),
+        functools.partial(scores_kernel, n_y, n_z),
         name="scores_and_tables",
         out_shape=(
-            jax.ShapeDtypeStruct((n_col, HEADS, chip), f32),
+            jax.ShapeDtypeStruct((n_y * n_z, HEADS, chip), f32),
             jax.ShapeDtypeStruct((2, HALF, chip), bf16),
             jax.ShapeDtypeStruct((2, HEADS, chip), f32),
             jax.ShapeDtypeStruct((1, ORDER), jnp.int32),
@@ -534,14 +546,15 @@
             pltpu.VMEM(tile_count.shape, jnp.int32), pltpu.VMEM(src_feat.shape, bf16),
             pltpu.VMEM((HEADS, chip), f32), pltpu.VMEM((HEADS, chip), f32), pltpu.VMEM((FEAT, chip), bf16),
             pltpu.VMEM((FEAT, weight.shape[0]), bf16), pltpu.VMEM((FEAT, TILE), f32),
-            DMA((8,)), DMA((n_col,)), DMA((n_col,)), DMA((2,)), DMA((2,)),
+            pltpu.VMEM((HEADS, chip), f32),
+            DMA((8,)), DMA((n_y - 1,)), DMA((n_y - 1,)), DMA((n_z - 1,)), DMA((n_z - 1,)), DMA((3,)), DMA((3,)),
         ],
         compiler_params=pltpu.CompilerParams(collective_id=0, has_side_effects=True, vmem_limit_bytes=40 * MIB),
     )(dst_feat, weight, att_src, att_dst, tile_rows, tile_cols, tile_count, src_feat)
 
 
 def edge_sums(order, pairs, scores, scaled, ratio, src_score, span, src_feat, weight, masks):
-    n_blocks = scores.shape[0] // 2
+    n_blocks = scores.shape[0]
     return pl.pallas_call(
         edges_kernel,
         name="edge_sums",
@@ -588,6 +601,8 @@
 
 
 def local(n_col, src_feat, dst_feat, weight, att_src, att_dst, bias, tile_rows, tile_cols, tile_masks, tile_count):
+    n_y = 4
+    n_z = n_col // (2 * n_y)
     slots = tile_rows.shape[2]
     tile_rows, tile_cols, bias = tile_rows.reshape(1, slots), tile_cols.reshape(1, slots), bias.reshape(1, FEAT)
     tile_masks = tile_masks.reshape(slots, TILE, TILE)
@@ -596,10 +611,9 @@
         for array in (src_feat, dst_feat, weight, att_src, att_dst, bias, tile_rows, tile_cols, tile_masks)
     ]
     scores, self_values, cross, order, pairs, scaled, ratio, src_score, span = scores_and_tables(
-        n_col, dst_feat, weight, att_src, att_dst, tile_rows, tile_cols, tile_count, src_feat)
+        n_y, n_z, dst_feat, weight, att_src, att_dst, tile_rows, tile_cols, tile_count, src_feat)
     parts = edge_sums(order, pairs, scores, scaled, ratio, src_score, span, src_feat, weight, tile_masks)
-    n_y = 4
-    return merge(n_y, n_col // (2 * n_y), parts, scores, self_values, cross, bias)
+    return merge(n_y, n_z, parts, scores, self_values, cross, bias)
 
 
 def solution(mesh):

time: 115 us -> 114 us (level)
    pallas_call x1, Pallas kernels: 37.7 us -> 64 us  [edge_sums(): pl.pallas_call(edges_kernel, name='edge_sums', out_shape=jax.ShapeDtypeSt...]
    pallas_call x1, Pallas kernels: 60.4 us -> 35.6 us  [merge(): pl.pallas_call(functools.partial(merge_kernel, n_y, n_z), name='merge', o...]
    pallas_call x1, Pallas kernels: 14.2 us -> 12.5 us  [scores_and_tables(): pl.pallas_call(functools.partial(scores_kernel, n_y, n_z), name='scores_a...]
where the time goes in v4:
time: 114 us; the launch traced here: 113 us
  Pallas kernels  112 us (98%)
    pallas_call x1, Pallas kernels, edge_sums(): pl.pallas_call(edges_kernel, name='edge_sums', out_shape=jax.ShapeDtypeSt...  64 us
    pallas_call x1, Pallas kernels, merge(): pl.pallas_call(functools.partial(merge_kernel, n_y, n_z), name='merge', o...  35.6 us
    pallas_call x1, Pallas kernels, scores_and_tables(): pl.pallas_call(functools.partial(scores_kernel, n_y, n_z), name='scores_a...  12.5 us

profile of v4, /device:TPU:7, one launch (start us, length us, event | category | flops | bytes accessed | tf_op | source)
XLA Modules:
  0.0 113.4 jit_solution(2017063578341609046)
XLA Ops:
  0.7 12.5 %scores_and_tables.1 = (f32[16,8,128]{2,1,0:T(8,128)S(1)}, bf16[2,256,128]{2,1,0:T(8,128)(2,1)S(1)}, f32[2,8,128]{2,1,0:T(8,128)S(1)}, s32[1,256]{1,0:T(1,128)S(...) custom-call(bf16[64,128]{1,0:T(8,128)(2,1)} %dst_hbm.1, ...), custom_call_target="tpu_custom_call" | custom-call | tf_op jit(solution)/shard_map/scores_and_tables/pallas_call | solution.py:526
  13.1 64.0 %edge_sums.1.part_ref = bf16[2,16,272,128]{3,2,1,0:T(8,128)(2,1)S(1)} custom-call(s32[1,256]{1,0:T(1,128)S(1)} %get-tuple-element.14.order_ref, s32[1,128]{1,0:T(1,128)S(1)} %get-tuple-element.15.pairs_ref, f32[16,8,128]{2,1,0:T(8,128)S(1)} %get-tuple-element.16.score_ref, bf16[32,8,80,128]{3,2,1,0:T(8,128)(2,1)S(1)} %get-tuple-element.17.scaled, ...), custom_call_target="tpu_custom_call" | custom-call | tf_op jit(solution)/shard_map/edge_sums/pallas_call | solution.py:558
  77.2 35.6 %merge.1 = f32[64,512]{1,0:T(8,128)S(1)} custom-call(bf16[2,16,272,128]{3,2,1,0:T(8,128)(2,1)S(1)} %edge_sums.1.part_ref, f32[16,8,128]{2,1,0:T(8,128)S(1)} %get-tuple-element.16.score_ref, bf16[2,256,128]{2,1,0:T(8,128)(2,1)S(1)} %get-tuple-element.21.self_ref, f32[2,8,128]{2,1,0:T(8,128)S(1)} %get-tuple-element.22.cross_ref, f32[1,512]{1,0:T(1,128)} %bitcast.5), custom_call_target="tpu_custom_call" | custom-call | tf_op jit(solution)/shard_map/merge/pallas_call | solution.py:580
  112.8 0.7 copy.13

commit v5 on v4

--- a/solution.py
+++ b/solution.py
@@ -238,18 +238,16 @@
     def mask_of(ring, side, code):
         return masks[ring, side].astype(f32) * jnp.minimum(code, 1).astype(f32)
 
-    def prefetch(pair, carry):
-        fetch(pair)
-        return carry
-
-    lax.fori_loop(0, jnp.minimum(groups * GROUP, RING - GROUP), prefetch, 0)
-
     spread_head = lax.broadcasted_iota(jnp.int32, (HEADS, HEADS * TILE), 0)
     spread_lane = lax.broadcasted_iota(jnp.int32, (HEADS, HEADS * TILE), 1) // TILE
     spread = jnp.where(spread_head == spread_lane, 1.0, 0.0).astype(bf16)
 
+    early = (RING - GROUP) // (n_blocks // 4)
+
     def dst_block(step, carry):
         low, high = carry
+        for first in range(early):
+            fetch(early * step + first)
         for part in range(4):
             block = 4 * step + part
             score = score_ref[block]
@@ -276,8 +274,12 @@
 
     @pl.when(factored)
     def _():
-        def group_step(group, carry):
-            next_group(group)
+        def group_step(more, group, carry):
+            for step in range(GROUP):
+                arrive(group * GROUP + step)
+            if more:
+                for step in range(GROUP):
+                    fetch(group * GROUP + step + RING - GROUP)
             one = jnp.ones((), bf16)
             for step in range(GROUP):
                 pair = group * GROUP + step
@@ -296,7 +298,9 @@
                                                      preferred_element_type=f32)
             return carry
 
-        lax.fori_loop(0, groups, group_step, 0)
+        last = groups - (RING - GROUP) // GROUP
+        lax.fori_loop(0, last, functools.partial(group_step, True), 0)
+        lax.fori_loop(last, groups, functools.partial(group_step, False), 0)
 
         def reference_rows(block, carry):
             for h in range(HEADS):
@@ -459,11 +463,11 @@
 
     def pair_merge(step):
         pair_copy(step).wait()
-        for dy in range(n_y):
+        for dy in (2, 1, 3, 0):
             block = z_of(step) * n_y + lax.rem(y + dy, n_y)
             store_block_parts(summed, (block,), merge_blocks([part_ref[core, block], pair_in[block]]))
-        for dy in range(1, n_y):
-            y_copy(step, dy).start()
+            if dy:
+                y_copy(step, dy).start()
 
     def y_merge(step):
         for dy in range(1, n_y):

time: 114 us -> 112 us (0.982)
    pallas_call x1, Pallas kernels: 64 us -> 24.3 us  [edge_sums(): pl.pallas_call(edges_kernel, name='edge_sums', out_shape=jax.ShapeDtypeSt...]
    pallas_call x1, Pallas kernels: 35.6 us -> 73.7 us  [merge(): pl.pallas_call(functools.partial(merge_kernel, n_y, n_z), name='merge', o...]
where the time goes in v5:
time: 112 us
  Pallas kernels  111 us (99%)
    pallas_call x1, Pallas kernels, merge(): pl.pallas_call(functools.partial(merge_kernel, n_y, n_z), name='merge', o...  73.7 us
    pallas_call x1, Pallas kernels, edge_sums(): pl.pallas_call(edges_kernel, name='edge_sums', out_shape=jax.ShapeDtypeSt...  24.3 us
    pallas_call x1, Pallas kernels, scores_and_tables(): pl.pallas_call(functools.partial(scores_kernel, n_y, n_z), name='scores_a...  12.5 us

profile of v5, /device:TPU:7, one launch (start us, length us, event | category | flops | bytes accessed | tf_op | source)
XLA Modules:
  0.0 111.8 jit_solution(1607477674948641958)
XLA Ops:
  0.7 12.5 %scores_and_tables.1 = (f32[16,8,128]{2,1,0:T(8,128)S(1)}, bf16[2,256,128]{2,1,0:T(8,128)(2,1)S(1)}, f32[2,8,128]{2,1,0:T(8,128)S(1)}, s32[1,256]{1,0:T(1,128)S(...) custom-call(bf16[64,128]{1,0:T(8,128)(2,1)} %dst_hbm.1, ...), custom_call_target="tpu_custom_call" | custom-call | tf_op jit(solution)/shard_map/scores_and_tables/pallas_call | solution.py:530
  13.1 24.3 %edge_sums.1.part_ref = bf16[2,16,272,128]{3,2,1,0:T(8,128)(2,1)S(1)} custom-call(s32[1,256]{1,0:T(1,128)S(1)} %get-tuple-element.14.order_ref, s32[1,128]{1,0:T(1,128)S(1)} %get-tuple-element.15.pairs_ref, f32[16,8,128]{2,1,0:T(8,128)S(1)} %get-tuple-element.16.score_ref, bf16[32,8,80,128]{3,2,1,0:T(8,128)(2,1)S(1)} %get-tuple-element.17.scaled, ...), custom_call_target="tpu_custom_call" | custom-call | tf_op jit(solution)/shard_map/edge_sums/pallas_call | solution.py:562
  37.5 73.7 %merge.1 = f32[64,512]{1,0:T(8,128)S(1)} custom-call(bf16[2,16,272,128]{3,2,1,0:T(8,128)(2,1)S(1)} %edge_sums.1.part_ref, f32[16,8,128]{2,1,0:T(8,128)S(1)} %get-tuple-element.16.score_ref, bf16[2,256,128]{2,1,0:T(8,128)(2,1)S(1)} %get-tuple-element.21.self_ref, f32[2,8,128]{2,1,0:T(8,128)S(1)} %get-tuple-element.22.cross_ref, f32[1,512]{1,0:T(1,128)} %bitcast.5), custom_call_target="tpu_custom_call" | custom-call | tf_op jit(solution)/shard_map/merge/pallas_call | solution.py:584
  111.2 0.7 copy.13
